TPU v7x, 256 devices: a whole 4x4x8 slice. The times are simulated.
256 devices in a mesh: segment: 2 (over core), chan: 128 (over y, x, z).
Axes of the slice: x: 4, y: 4, z: 8, core: 2. Of those that a mesh axis runs over, the one named last changes fastest.
Arguments:
- records: bfloat16 [4, 10240, 7680], P(None, 'chan')
- fan_limit: int32 [512], replicated, may hold values from 1 to 5120, as said below
- sources: int32 [256], replicated, may hold values from 0 to 10239, as said below
Outputs:
- correlations: bfloat16 [256, 1024, 512], P('segment', 'chan')
Inputs may be any that keep to these rules, and one draw needn't show every extreme that they name: `sources`: 256 distinct channel indices; 0 and 10239 are among them. `fan_limit`: one limit for each band bin; the limits 1 and 5120 both occur.
All inputs are finite; a program needn't handle non-finite values.
Results may differ from a plain program's by a relative error of at most 0.0085.
Values may be sent and summed in bfloat16 or wider, within the bound.
A program may use at most 192 MiB of HBM per device.

v0:
```python
import functools
import math

import jax
import jax.numpy as jnp
import numpy as np
from jax import lax
from jax.experimental import pallas as pl
from jax.experimental.pallas import tpu as pltpu
from jax.sharding import PartitionSpec as P

NCH = 10240
NT = 7680
NF = 512
FLO = 32
NVS = 256
STRIDE = 10
LAGS = 512
MB = 4

epsilon = 1e-06

SEG = 2
NY, NX, NZ = 4, 4, 8
CHIPS = NY * NX * NZ
CH_DEV = NCH // CHIPS
F_DEV = NF // CHIPS
M_DEV = MB // SEG
SEQS = F_DEV * M_DEV
RECS = CH_DEV // STRIDE
HALF = NVS // SEG
LANES = 128
WIDE = SEQS * CH_DEV
KBLOCK = 1280
MESH = pl.DeviceIdType.MESH
BF = jnp.bfloat16
F32 = jnp.float32


def as_bf16(array):
    return np.asarray(array, np.float32).astype(jnp.bfloat16)


def split(array):
    high = as_bf16(array)
    low = as_bf16(np.asarray(array, np.float64) - high.astype(np.float64))
    return high, low


def time_table():
    freqs = FLO + np.arange(NF, dtype=np.int64)
    phase = freqs[:, None] * np.arange(NT, dtype=np.int64)[None, :] % NT
    angle = phase.astype(np.float32) * np.float32(2.0 * math.pi / NT)
    return as_bf16(np.concatenate([np.cos(angle), -np.sin(angle)], axis=0))


def lag_table():
    lagged = np.arange(LAGS, dtype=np.int64) - LAGS // 2
    freqs = FLO + np.arange(NF, dtype=np.int64)
    phase = freqs[:, None] * lagged[None, :] % NT
    angle = phase.astype(np.float32) * np.float32(2.0 * math.pi / NT)
    return as_bf16(np.concatenate([np.cos(angle), -np.sin(angle)], axis=0))


def roots(rows, cols, modulus):
    phase = np.arange(rows)[:, None] * np.arange(cols)[None, :] % modulus
    angle = phase * (2.0 * math.pi / modulus)
    return np.cos(angle), -np.sin(angle)


def filter_tables():
    dr, di = roots(CHIPS, CHIPS, CHIPS)
    er = np.zeros((LANES, LANES))
    ei = np.zeros((LANES, LANES))
    er[:CH_DEV, :CH_DEV], ei[:CH_DEV, :CH_DEV] = roots(CH_DEV, CH_DEV, CH_DEV)
    tr = np.zeros((CHIPS, LANES))
    ti = np.zeros((CHIPS, LANES))
    tr[:, :CH_DEV], ti[:, :CH_DEV] = roots(CHIPS, CH_DEV, NCH)
    outer = np.block([[dr, -di], [di, dr]])
    inner = np.block([[er, ei], [-ei, er]])
    inner_back = np.block([[er, -ei], [ei, er]])
    outer_back = np.block([[dr, di], [-di, dr]])
    tables = np.stack([t for m in (outer, inner, inner_back, outer_back) for t in split(m)])
    twist = np.stack([tr, ti]).astype(np.float32)
    pick = np.zeros((2, SEQS, LANES, LANES), np.float32)
    for part in range(2):
        for q in range(SEQS):
            for u in range(RECS):
                pick[part, q, STRIDE * u, (q * 2 + part) * RECS + u] = 1.0
    return tables, twist, as_bf16(pick.reshape(2, SEQS * LANES, LANES))


def mm(left, right):
    return jnp.dot(left, right, preferred_element_type=F32)


def mm_nt(left, right):
    return lax.dot_general(left, right, (((1,), (1,)), ((), ())), preferred_element_type=F32)


def halves(value):
    high = value.astype(BF)
    return high, (value - high.astype(F32)).astype(BF)


def transform_kernel(seg_ref, rec_ref, table_ref, out_ref, acc):
    step = pl.program_id(0)
    piece = rec_ref[...].reshape(M_DEV * CH_DEV, KBLOCK)
    part = mm_nt(table_ref[...], piece)

    @pl.when(step == 0)
    def _():
        acc[...] = part

    @pl.when(step > 0)
    def _():
        acc[...] += part

    @pl.when(step == NT // KBLOCK - 1)
    def _():
        spectra = acc[...] * (1.0 / math.sqrt(NT))
        power = jnp.sum(spectra * spectra, axis=0, keepdims=True) * (1.0 / NF)
        white = spectra * lax.rsqrt(power + epsilon)
        blocks = [white[CHIPS * g : CHIPS * (g + 1)] for g in range(2 * F_DEV)]
        out_ref[...] = jnp.concatenate(blocks, axis=1).astype(BF)


def transform(records, table):
    segment = lax.axis_index("segment").astype(jnp.int32).reshape(1)
    return pl.pallas_call(
        transform_kernel,
        out_shape=jax.ShapeDtypeStruct((CHIPS, 2 * WIDE), BF),
        grid_spec=pltpu.PrefetchScalarGridSpec(
            num_scalar_prefetch=1,
            grid=(NT // KBLOCK,),
            in_specs=[
                pl.BlockSpec((M_DEV, CH_DEV, KBLOCK), lambda k, seg: (seg[0], 0, k)),
                pl.BlockSpec((2 * NF, KBLOCK), lambda k, seg: (0, k)),
            ],
            out_specs=pl.BlockSpec((CHIPS, 2 * WIDE), lambda k, seg: (0, 0)),
            scratch_shapes=[pltpu.VMEM((2 * NF, M_DEV * CH_DEV), F32)],
        ),
        compiler_params=pltpu.CompilerParams(vmem_limit_bytes=40 << 20),
        cost_estimate=pl.CostEstimate(
            flops=2 * 2 * NF * NT * M_DEV * CH_DEV, bytes_accessed=18 << 20, transcendentals=0
        ),
        name="transform",
    )(segment, records, table)


def filter_kernel(col_ref, limit_ref, src_ref, x_ref, tables, twist, pick, s_ref, r_ref):
    column = col_ref[0]
    x = x_ref[...]
    tail = jnp.zeros((CHIPS, LANES), BF)
    xs = jnp.concatenate(
        [
            jnp.concatenate([x[:, :WIDE], tail], axis=1),
            jnp.concatenate([x[:, WIDE:], tail], axis=1),
        ],
        axis=0,
    )
    first = mm(tables[0], xs) + mm(tables[1], xs)
    tr, ti = twist[0], twist[1]
    turned = []
    for q in range(SEQS):
        yr = first[:CHIPS, CH_DEV * q : CH_DEV * q + LANES]
        yi = first[CHIPS:, CH_DEV * q : CH_DEV * q + LANES]
        turned.append(jnp.concatenate([yr * tr - yi * ti, yr * ti + yi * tr], axis=1))
    high, low = halves(jnp.concatenate(turned, axis=0))
    wave = mm(high, tables[2]) + mm(high, tables[3]) + mm(low, tables[2])
    shape = (CHIPS, 2 * LANES)
    lane = lax.broadcasted_iota(jnp.int32, shape, 1) % LANES
    index = lax.broadcasted_iota(jnp.int32, shape, 0) + CHIPS * lane
    signed = jnp.where(index < NCH // 2, index, index - NCH)
    reach = jnp.where(index < NCH, jnp.abs(signed), NCH)
    kept = []
    for q in range(SEQS):
        limit = limit_ref[(q // M_DEV) * CHIPS + column]
        kept.append(jnp.where(reach <= limit, wave[CHIPS * q : CHIPS * (q + 1)], 0.0))
    high, low = halves(jnp.concatenate(kept, axis=0))
    back = mm(high, tables[4]) + mm(high, tables[5]) + mm(low, tables[4])
    real, imag = [], []
    for q in range(SEQS):
        ur = back[CHIPS * q : CHIPS * (q + 1), :LANES]
        ui = back[CHIPS * q : CHIPS * (q + 1), LANES:]
        real.append(ur * tr + ui * ti)
        imag.append(ui * tr - ur * ti)
    high, low = halves(
        jnp.concatenate([jnp.concatenate(real, axis=1), jnp.concatenate(imag, axis=1)], axis=0)
    )
    field = mm(tables[6], high) + mm(tables[6], low) + mm(tables[7], high)
    field = (field * (1.0 / NCH)).astype(BF)
    r_ref[...] = mm(field[:CHIPS], pick[0]) + mm(field[CHIPS:], pick[1])
    source = src_ref[...]
    chip = ((source.astype(F32) + 0.5) * (1.0 / CH_DEV)).astype(jnp.int32)
    inside = source - CH_DEV * chip
    rows = lax.broadcasted_iota(jnp.int32, (LANES, NVS), 0)
    hot_inside = jnp.where(rows == inside, 1.0, 0.0).astype(BF)
    hot_chip = jnp.where(rows == chip, 1.0, 0.0)
    lines = []
    for q in range(SEQS):
        for part in range(2):
            block = field[CHIPS * part : CHIPS * (part + 1), LANES * q : LANES * (q + 1)]
            chosen = mm(block, hot_inside) * hot_chip
            lines.append(jnp.sum(chosen, axis=0, keepdims=True))
    found = jnp.concatenate(lines, axis=0).astype(BF)
    s_ref[0] = found[:, :HALF]
    s_ref[1] = found[:, HALF:]


def fan_filter(mixed, limits, sources):
    tables, twist, pick = filter_tables()
    column = lax.axis_index("chan").astype(jnp.int32).reshape(1)
    smem = pl.BlockSpec(memory_space=pltpu.SMEM)
    vmem = pl.BlockSpec(memory_space=pltpu.VMEM)
    return pl.pallas_call(
        filter_kernel,
        out_shape=(
            jax.ShapeDtypeStruct((SEG, 2 * SEQS, HALF), BF),
            jax.ShapeDtypeStruct((CHIPS, LANES), F32),
        ),
        in_specs=[smem, smem, vmem, vmem, vmem, vmem, vmem],
        out_specs=(vmem, vmem),
        compiler_params=pltpu.CompilerParams(vmem_limit_bytes=40 << 20),
        cost_estimate=pl.CostEstimate(flops=4 << 30, bytes_accessed=4 << 20, transcendentals=0),
        name="fan_filter",
    )(
        column,
        limits,
        sources.reshape(1, NVS),
        mixed,
        jnp.asarray(tables),
        jnp.asarray(twist),
        jnp.asarray(pick),
    )


def spread_kernel(s_in, r_in, s_all, r_fin, rz, rx, sz_s, sz_r, sx_s, sx_r, sy_s, sy_r, rz_s, rz_r,
                  rx_s, rx_r, ry_s, ry_r, here):
    seg = lax.axis_index("segment")
    chan = lax.axis_index("chan")
    z = lax.rem(chan, NZ)
    plane = lax.div(chan, NZ)
    x = lax.rem(plane, NX)
    y = lax.div(plane, NX)

    def target(ds, dy, dx, dz):
        ty, tx, tz = lax.rem(y + dy, NY), lax.rem(x + dx, NX), lax.rem(z + dz, NZ)
        return (lax.rem(seg + ds, SEG), (ty * NX + tx) * NZ + tz)

    def remote(src, dst, send, recv, device):
        return pltpu.make_async_remote_copy(
            src_ref=src, dst_ref=dst, send_sem=send, recv_sem=recv,
            device_id=device, device_id_type=MESH,
        )

    peers = [(ds, 0, 0, dz) for ds in range(SEG) for dz in range(NZ) if ds or dz]
    peers += [(0, 0, dx, 0) for dx in range(1, NX)]
    peers += [(ds, dy, 0, 0) for ds in range(SEG) for dy in range(1, NY)]
    barrier = pltpu.get_barrier_semaphore()
    for peer in peers:
        pl.semaphore_signal(barrier, inc=1, device_id=target(*peer), device_id_type=MESH)
    pl.semaphore_wait(barrier, len(peers))

    own_s = pltpu.make_async_copy(s_in.at[seg], s_all.at[seg, y, x, z], here.at[0])
    own_z = pltpu.make_async_copy(r_in.at[:, :, z], rz.at[z], here.at[1])
    own_s.start()
    own_z.start()
    s_z, r_z = [], []
    for ds in range(SEG):
        for dz in range(NZ):
            if ds or dz:
                k = ds * NZ + dz
                s_z.append(remote(s_in.at[lax.rem(seg + ds, SEG)], s_all.at[seg, y, x, z],
                                  sz_s.at[k], sz_r.at[k], target(ds, 0, 0, dz)))
    for dz in range(1, NZ):
        r_z.append(remote(r_in.at[:, :, lax.rem(z + dz, NZ)], rz.at[z],
                          rz_s.at[dz], rz_r.at[dz], target(0, 0, 0, dz)))
    for copy in s_z + r_z:
        copy.start()
    own_s.wait()
    for copy in s_z:
        copy.wait_recv()
    s_x = []
    for d in range(1, NX):
        s_x.append(remote(s_all.at[0, y, x], s_all.at[0, y, x],
                          sx_s.at[0, d], sx_r.at[0, d], target(0, 0, d, 0)))
        s_x.append(remote(s_all.at[1, y, x], s_all.at[1, y, x],
                          sx_s.at[1, d], sx_r.at[1, d], target(0, d, 0, 0)))
    for copy in s_x:
        copy.start()
    own_z.wait()
    for copy in r_z:
        copy.wait_recv()
    own_x = pltpu.make_async_copy(rz.at[:, :, x], rx.at[x], here.at[2])
    own_x.start()
    r_x = []
    for d in range(1, NX):
        r_x.append(remote(rz.at[:, :, lax.rem(x + d, NX)], rx.at[x],
                          rx_s.at[d], rx_r.at[d], target(0, 0, d, 0)))
    for copy in r_x:
        copy.start()
    for copy in s_x:
        copy.wait_recv()
    s_y = []
    for d in range(1, NY):
        s_y.append(remote(s_all.at[0, y], s_all.at[0, y],
                          sy_s.at[0, d], sy_r.at[0, d], target(0, d, 0, 0)))
        s_y.append(remote(s_all.at[1, :, x], s_all.at[1, :, x],
                          sy_s.at[1, d], sy_r.at[1, d], target(0, 0, d, 0)))
    for copy in s_y:
        copy.start()
    own_x.wait()
    for copy in r_x:
        copy.wait_recv()
    own_y = pltpu.make_async_copy(rx.at[:, :, y], r_fin.at[seg, y], here.at[3])
    own_y.start()
    r_y = []
    for ds in range(SEG):
        for d in range(NY):
            if ds or d:
                k = ds * NY + d
                r_y.append(remote(rx.at[:, :, lax.rem(y + d, NY)], r_fin.at[seg, y],
                                  ry_s.at[k], ry_r.at[k], target(ds, d, 0, 0)))
    for copy in r_y:
        copy.start()
    own_y.wait()
    for copy in s_y + r_y:
        copy.wait_recv()
    for copy in s_z + r_z + s_x + r_x + s_y + r_y:
        copy.wait_send()


def spread(s_loc, r_loc):
    vmem = pl.BlockSpec(memory_space=pltpu.VMEM)
    dma = pltpu.SemaphoreType.DMA
    return pl.pallas_call(
        spread_kernel,
        out_shape=(
            jax.ShapeDtypeStruct((SEG, NY, NX, NZ, 2 * SEQS, HALF), BF),
            jax.ShapeDtypeStruct((SEG, NY, NX, NZ, 1, LANES), F32),
        ),
        in_specs=[vmem, vmem],
        out_specs=(vmem, vmem),
        scratch_shapes=[
            pltpu.VMEM((NZ, NY, NX, 1, LANES), F32),
            pltpu.VMEM((NX, NZ, NY, 1, LANES), F32),
            dma((SEG * NZ,)), dma((SEG * NZ,)),
            dma((2, NX)), dma((2, NX)),
            dma((2, NY)), dma((2, NY)),
            dma((NZ,)), dma((NZ,)),
            dma((NX,)), dma((NX,)),
            dma((SEG * NY,)), dma((SEG * NY,)),
            dma((4,)),
        ],
        compiler_params=pltpu.CompilerParams(
            collective_id=0, has_side_effects=True, vmem_limit_bytes=24 << 20
        ),
        name="spread",
    )(s_loc, r_loc.reshape(NY, NX, NZ, 1, LANES))


VBLOCK = 32


def correlate_kernel(s_ref, r_ref, lag_ref, out_ref, flat, st, rt, cross):
    step = pl.program_id(0)

    @pl.when(step == 0)
    def _():
        shape = (LANES, LANES)
        eye = lax.broadcasted_iota(jnp.int32, shape, 0) == lax.broadcasted_iota(jnp.int32, shape, 1)
        eye = jnp.where(eye, 1.0, 0.0).astype(BF)
        for h in range(SEG):
            rt[h] = mm_nt(eye, r_ref[h].astype(BF))
            flat[...] = s_ref[h].reshape(CHIPS * 2 * SEQS, HALF).astype(F32)
            for g in range(2 * SEQS):
                piece = flat[pl.ds(g, CHIPS, stride=2 * SEQS), :].astype(BF)
                st[h, g] = mm_nt(eye, piece)

    for f in range(F_DEV):
        rr, ri = [], []
        for h in range(SEG):
            for m in range(M_DEV):
                g = (f * M_DEV + m) * 2
                rr.append(rt[h, RECS * g : RECS * (g + 1)])
                ri.append(rt[h, RECS * (g + 1) : RECS * (g + 2)])

        def body(b, carry, f=f, rr=rr, ri=ri):
            rows = pl.ds(pl.multiple_of(step * VBLOCK + b * 8, 8), 8)
            cr = jnp.zeros((8, RECS, LANES), F32)
            ci = jnp.zeros((8, RECS, LANES), F32)
            for h in range(SEG):
                for m in range(M_DEV):
                    g = (f * M_DEV + m) * 2
                    sr = st[h, g, rows, :][:, None, :]
                    si = st[h, g + 1, rows, :][:, None, :]
                    r, i = rr[h * M_DEV + m][None], ri[h * M_DEV + m][None]
                    cr = cr + sr * r + si * i
                    ci = ci + sr * i - si * r
            to = pl.ds(pl.multiple_of(b * 8 * RECS, 8 * RECS), 8 * RECS)
            cross[to, f * LANES : (f + 1) * LANES] = cr.reshape(8 * RECS, LANES).astype(BF)
            cross[to, NF + f * LANES : NF + (f + 1) * LANES] = (
                ci.reshape(8 * RECS, LANES).astype(BF)
            )
            return carry

        lax.fori_loop(0, VBLOCK // 8, body, 0, unroll=True)
    result = mm(cross[...], lag_ref[...]) * (1.0 / math.sqrt(MB * NF))
    out_ref[...] = result.astype(BF).reshape(VBLOCK, RECS, LAGS)


def correlate(s_all, r_all):
    return pl.pallas_call(
        correlate_kernel,
        out_shape=jax.ShapeDtypeStruct((HALF, RECS, LAGS), BF),
        grid=(HALF // VBLOCK,),
        in_specs=[
            pl.BlockSpec((SEG, CHIPS, 2 * SEQS, HALF), lambda k: (0, 0, 0, 0)),
            pl.BlockSpec((SEG, CHIPS, LANES), lambda k: (0, 0, 0)),
            pl.BlockSpec((2 * NF, LAGS), lambda k: (0, 0)),
        ],
        out_specs=pl.BlockSpec((VBLOCK, RECS, LAGS), lambda k: (k, 0, 0)),
        scratch_shapes=[
            pltpu.VMEM((CHIPS * 2 * SEQS, HALF), F32),
            pltpu.VMEM((SEG, 2 * SEQS, HALF, CHIPS), F32),
            pltpu.VMEM((SEG, LANES, CHIPS), F32),
            pltpu.VMEM((VBLOCK * RECS, 2 * NF), BF),
        ],
        compiler_params=pltpu.CompilerParams(vmem_limit_bytes=40 << 20),
        cost_estimate=pl.CostEstimate(flops=3 << 30, bytes_accessed=4 << 20, transcendentals=0),
        name="correlate",
    )(s_all, r_all, jnp.asarray(lag_table()))


def shards(records, fan_limit, sources):
    white = transform(records, jnp.asarray(time_table()))
    mixed = lax.all_to_all(white, "chan", split_axis=0, concat_axis=0, tiled=True)
    s_loc, r_loc = fan_filter(mixed, fan_limit, sources)
    s_all, r_all = spread(s_loc, r_loc)
    return correlate(
        s_all.reshape(SEG, CHIPS, 2 * SEQS, HALF), r_all.reshape(SEG, CHIPS, LANES)
    )


def solution(mesh):
    in_specs = (P(None, "chan", None), P(), P())
    out_specs = P("segment", "chan", None)
    return jax.shard_map(shards, mesh=mesh, in_specs=in_specs, out_specs=out_specs, check_vma=False)
```

profile of v0, /device:TPU:1, one launch (start us, length us, event | category | flops | bytes accessed | tf_op | source)
XLA Modules:
  0.0 84.9 jit_solution(15238891150172876918)
XLA Ops:
  0.0 0.0 copy-start.2
  0.0 0.0 copy-start.1
  0.0 0.0 copy-start
  0.0 2.4 %copy-done = bf16[4,80,7680]{2,1,0:T(8,128)(2,1)S(1)} copy-done((bf16[4,80,7680]{2,1,0:T(8,128)(2,1)S(1)}, bf16[4,80,7680]{2,1,0:T(8,128)(2,1)}, u32[]{:S(2)}) %copy-start) | copy-done | bytes 4915224
  2.4 0.0 copy-start.4
  2.4 0.0 copy-start.5
  2.4 0.0 copy-start.6
  2.4 0.0 copy-start.3
  2.4 10.0 %transform.1 = bf16[128,1280]{1,0:T(8,128)(2,1)S(1)} custom-call(s32[1]{0:T(128)} %bitcast.2.seg_ref, bf16[4,80,7680]{2,1,0:T(8,128)(2,1)S(1)} %copy-done, bf16[1024,7680]{1,0:T(8,128)(2,1)} %constant.19.clone.table_ref), custom_call_target="tpu_custom_call" | custom-call | flops 2516582400 | bytes 18874368 | tf_op jit(solution)/shard_map/transform/pallas_call | solution.py:130
  12.4 0.5 broadcast
  13.0 0.8 reduce
  13.8 0.8 reshape.26
  14.6 16.8 %all-to-all-start = ((bf16[128,2,640]{2,1,0:T(2,128)(2,1)}), bf16[128,2,640]{2,1,0:T(2,128)(2,1)}, u32[]{:S(2)}, u32[]{:S(2)}) async-start(bf16[128,2,640]{2,1,0:T(2,128)(2,1)} %reshape.26), calls=%async_computation | async-start | bytes 655360 | tf_op jit(solution)/shard_map/all_to_all | solution.py:438
  31.4 14.7 %all-to-all-done = bf16[128,2,640]{2,1,0:T(2,128)(2,1)} async-done(((bf16[128,2,640]{2,1,0:T(2,128)(2,1)}), bf16[128,2,640]{2,1,0:T(2,128)(2,1)}, u32[]{:S(2)}, u32[]{:S(2)}) %all-to-all-start) | async-done | bytes 327712 | tf_op jit(solution)/shard_map/all_to_all | solution.py:438
  46.1 2.5 %reshape.27 = bf16[128,1,1280]{2,1,0:T(2,128)(2,1)S(1)} reshape(bf16[128,2,640]{2,1,0:T(2,128)(2,1)} %all-to-all-done) | data formatting | bytes 655360
  48.7 0.0 copy-done.2
  48.7 0.0 copy-done.1
  48.7 0.0 copy-done.4
  48.7 0.0 copy-done.5
  48.7 0.0 copy-done.6
  48.7 4.0 %fan_filter.1 = (bf16[2,16,128]{2,1,0:T(8,128)(2,1)S(1)}, f32[128,128]{1,0:T(8,128)S(1)}) custom-call(s32[1]{0:T(128)} %bitcast.col_ref, s32[512]{0:T(512)S(1)} %copy-done.1, s32[1,256]{1,0:T(1,128)S(1)} %bitcast.15, bf16[128,1280]{1,0:T(8,128)(2,1)S(1)} %bitcast.11, bf16[8,256,256]{2,1,0:T(8,128)(2,1)S(1)} %copy-done.4, f32[2,128,128]{2,1,0:T(8,128)S(1)} %copy-done.6, ...), custom_call_target="tpu_custom_call" | custom-call | flops 4294967296 | bytes 4194304 | tf_op jit(solution)/shard_map/fan_filter/pallas_call | solution.py:216
  52.7 25.0 %spread.1 = (bf16[2,4,4,8,16,128]{5,4,3,2,1,0:T(8,128)(2,1)S(1)}, f32[2,4,4,8,1,128]{5,4,3,2,1,0:T(1,128)S(1)}) custom-call(bf16[2,16,128]{2,1,0:T(8,128)(2,1)S(1)} %get-tuple-element.9.s_in, f32[4,4,8,1,128]{4,3,2,1,0:T(1,128)S(1)} %bitcast.12), custom_call_target="tpu_custom_call" | custom-call | tf_op jit(solution)/shard_map/spread/pallas_call | solution.py:337
  77.7 0.0 copy-done.3
  77.7 7.2 %correlate.1 = bf16[128,8,512]{2,1,0:T(8,128)(2,1)} custom-call(bf16[2,128,16,128]{3,2,1,0:T(8,128)(2,1)S(1)} %bitcast.13, f32[2,128,128]{2,1,0:T(8,128)S(1)} %bitcast.14, bf16[1024,512]{1,0:T(8,128)(2,1)S(1)} %copy-done.3), custom_call_target="tpu_custom_call" | custom-call | flops 3221225472 | bytes 4194304 | tf_op jit(solution)/shard_map/correlate/pallas_call | solution.py:414
  (1 shorter events, 0.0 us)
Async XLA Ops:
  0.0 48.7 %copy-start.2 = (s32[256]{0:T(256)S(1)}, s32[256]{0:T(256)}, u32[]{:S(2)}) copy-start(s32[256]{0:T(256)} %param.10) | copy-start | bytes 3076
  0.0 48.7 %copy-start.1 = (s32[512]{0:T(512)S(1)}, s32[512]{0:T(512)}, u32[]{:S(2)}) copy-start(s32[512]{0:T(512)} %limit_ref.1) | copy-start | bytes 6148
  0.0 2.4 %copy-start = (bf16[4,80,7680]{2,1,0:T(8,128)(2,1)S(1)}, bf16[4,80,7680]{2,1,0:T(8,128)(2,1)}, u32[]{:S(2)}) copy-start(bf16[4,80,7680]{2,1,0:T(8,128)(2,1)} %rec_ref.1) | copy-start | bytes 14745604
  2.4 46.3 %copy-start.4 = (bf16[8,256,256]{2,1,0:T(8,128)(2,1)S(1)}, bf16[8,256,256]{2,1,0:T(8,128)(2,1)}, u32[]{:S(2)}) copy-start(bf16[8,256,256]{2,1,0:T(8,128)(2,1)} %constant.20.clone.tables) | copy-start | bytes 3145732
  2.4 46.3 %copy-start.5 = (bf16[2,1024,128]{2,1,0:T(8,128)(2,1)S(1)}, bf16[2,1024,128]{2,1,0:T(8,128)(2,1)}, u32[]{:S(2)}) copy-start(bf16[2,1024,128]{2,1,0:T(8,128)(2,1)} %constant.22.clone.pick) | copy-start | bytes 1572868
  2.4 46.3 %copy-start.6 = (f32[2,128,128]{2,1,0:T(8,128)S(1)}, f32[2,128,128]{2,1,0:T(8,128)}, u32[]{:S(2)}) copy-start(f32[2,128,128]{2,1,0:T(8,128)} %constant.21.clone.twist) | copy-start | bytes 393220
  2.4 75.3 %copy-start.3 = (bf16[1024,512]{1,0:T(8,128)(2,1)S(1)}, bf16[1024,512]{1,0:T(8,128)(2,1)}, u32[]{:S(2)}) copy-start(bf16[1024,512]{1,0:T(8,128)(2,1)} %constant.23.clone.lag_ref) | copy-start | bytes 3145732
  14.6 31.5 %all-to-all-start = ((bf16[128,2,640]{2,1,0:T(2,128)(2,1)}), bf16[128,2,640]{2,1,0:T(2,128)(2,1)}, u32[]{:S(2)}, u32[]{:S(2)}) async-start(bf16[128,2,640]{2,1,0:T(2,128)(2,1)} %reshape.26), calls=%async_computation | async-start | bytes 655360 | tf_op jit(solution)/shard_map/all_to_all | solution.py:438
where the time goes:
time: 85.2 us; the launch traced here: 84.9 us
  Pallas kernels  46.1 us (54%)
  starting transfers between devices  16.8 us (20%)
  waiting for transfers between devices  14.7 us (17%)
  local copies, waits for them, and re-layouts  6.26 us (7%)
    pallas_call x1, Pallas kernels, spread(): pl.pallas_call(spread_kernel, out_shape=(jax.ShapeDtypeStruct((SEG, NY, N...  25 us
    all_to_all x1, starting transfers between devices, shards(): lax.all_to_all(white, 'chan', split_axis=0, concat_axis=0, tiled=True)  16.8 us
    all_to_all x1, waiting for transfers between devices, shards(): lax.all_to_all(white, 'chan', split_axis=0, concat_axis=0, tiled=True)  14.7 us
    pallas_call x1, Pallas kernels, transform(): pl.pallas_call(transform_kernel, out_shape=jax.ShapeDtypeStruct((CHIPS, 2...  10 us
    pallas_call x1, Pallas kernels, correlate(): pl.pallas_call(correlate_kernel, out_shape=jax.ShapeDtypeStruct((HALF, RE...  7.18 us
    unnamed x17, local copies, waits for them, and re-layouts  5.74 us
    pallas_call x1, Pallas kernels, fan_filter(): pl.pallas_call(filter_kernel, out_shape=(jax.ShapeDtypeStruct((SEG, 2 * S...  3.95 us
  transfers between devices with their start and end apart: 1, of which 1 were waited for; matrix products, arithmetic and copies ran while one was open for 0% of the time, Pallas kernels for 0%

commit v1 on v0

v1 whole, which is shorter than its diff:
```python
import functools
import math

import jax
import jax.numpy as jnp
import numpy as np
from jax import lax
from jax.experimental import pallas as pl
from jax.experimental.pallas import tpu as pltpu
from jax.sharding import PartitionSpec as P

NCH = 10240
NT = 7680
NF = 512
FLO = 32
NVS = 256
STRIDE = 10
LAGS = 512
MB = 4

epsilon = 1e-06

SEG = 2
NY, NX, NZ = 4, 4, 8
CHIPS = NY * NX * NZ
CH_DEV = NCH // CHIPS
F_DEV = NF // CHIPS
M_DEV = MB // SEG
SEQS = F_DEV * M_DEV
RECS = CH_DEV // STRIDE
HALF = NVS // SEG
LANES = 128
HALF_SEQS = SEQS // 2
WIDE = HALF_SEQS * CH_DEV
PLANE = NY * NX
RADIX = 4
STEPS = 3
QUARTER = NT // RADIX
KBLOCK = QUARTER // STEPS
ROWS = M_DEV * CH_DEV
MESH = pl.DeviceIdType.MESH
BF = jnp.bfloat16
F32 = jnp.float32


def as_bf16(array):
    return np.asarray(array, np.float32).astype(jnp.bfloat16)


def split(array):
    high = as_bf16(array)
    low = as_bf16(np.asarray(array, np.float64) - high.astype(np.float64))
    return high, low


def time_tables():
    plane, late = np.meshgrid(np.arange(PLANE), np.arange(NZ // RADIX))
    chips = plane * NZ + RADIX * late
    bins = FLO + CHIPS * np.arange(F_DEV)[:, None] + chips.reshape(1, -1)
    times = np.arange(QUARTER, dtype=np.int64)
    columns = []
    for residue in (0, 2, 1, 3):
        freqs = (bins + residue).reshape(-1)
        phase = freqs[:, None] * times[None, :] % NT
        angle = phase.astype(np.float32) * np.float32(2.0 * math.pi / NT)
        cosine, sine = np.cos(angle), np.sin(angle)
        columns.append(np.concatenate([cosine, -sine], axis=0))
        if residue % 2:
            turn = 1.0 if residue == 3 else -1.0
            columns.append(np.concatenate([turn * sine, turn * cosine], axis=0))
    table = np.stack(columns, axis=1).reshape(2 * CHIPS, 6, STEPS, KBLOCK)
    return as_bf16(table.transpose(2, 0, 1, 3).reshape(STEPS, 2 * CHIPS, 6 * KBLOCK))


def lag_table():
    lagged = np.arange(LAGS, dtype=np.int64) - LAGS // 2
    freqs = FLO + np.arange(NF, dtype=np.int64)
    phase = freqs[:, None] * lagged[None, :] % NT
    angle = phase.astype(np.float32) * np.float32(2.0 * math.pi / NT)
    return as_bf16(np.concatenate([np.cos(angle), -np.sin(angle)], axis=0))


def roots(rows, cols, modulus):
    phase = np.arange(rows)[:, None] * np.arange(cols)[None, :] % modulus
    angle = phase * (2.0 * math.pi / modulus)
    return np.cos(angle), -np.sin(angle)


def filter_tables():
    dr, di = roots(CHIPS, CHIPS, CHIPS)
    er = np.zeros((LANES, LANES))
    ei = np.zeros((LANES, LANES))
    er[:CH_DEV, :CH_DEV], ei[:CH_DEV, :CH_DEV] = roots(CH_DEV, CH_DEV, CH_DEV)
    tr = np.zeros((CHIPS, LANES))
    ti = np.zeros((CHIPS, LANES))
    tr[:, :CH_DEV], ti[:, :CH_DEV] = roots(CHIPS, CH_DEV, NCH)
    outer = np.block([[dr, -di], [di, dr]])
    inner = np.block([[er, ei], [-ei, er]])
    inner_back = np.block([[er, -ei], [ei, er]])
    outer_back = np.block([[dr, di], [-di, dr]])
    major = np.arange(CHIPS).reshape(PLANE, NZ).T.reshape(-1)
    outer_z = np.block([[dr[:, major], -di[:, major]], [di[:, major], dr[:, major]]])
    order = (outer, inner, inner_back, outer_back, outer_z)
    tables = np.stack([t for m in order for t in split(m)])
    twist = np.stack([tr, ti]).astype(np.float32)
    pick = np.zeros((2, SEQS, LANES, LANES), np.float32)
    for part in range(2):
        for q in range(SEQS):
            for u in range(RECS):
                pick[part, q, STRIDE * u, (q * 2 + part) * RECS + u] = 1.0
    return tables, twist, as_bf16(pick.reshape(2, SEQS * LANES, LANES))


def mm(left, right):
    return jnp.dot(left, right, preferred_element_type=F32)


def mm_nt(left, right):
    return lax.dot_general(left, right, (((1,), (1,)), ((), ())), preferred_element_type=F32)


def halves(value):
    high = value.astype(BF)
    return high, (value - high.astype(F32)).astype(BF)


def filter_half(h, x, column, limit_ref, tables, twist):
    tail = jnp.zeros((CHIPS, LANES // 2), BF)
    xs = jnp.concatenate(
        [
            jnp.concatenate([x[:, :WIDE], tail], axis=1),
            jnp.concatenate([x[:, WIDE:], tail], axis=1),
        ],
        axis=0,
    )
    outer = 0 if h == 0 else 8
    first = mm(tables[outer], xs) + mm(tables[outer + 1], xs)
    tr, ti = twist[0], twist[1]
    turned = []
    for q in range(HALF_SEQS):
        yr = first[:CHIPS, CH_DEV * q : CH_DEV * q + LANES]
        yi = first[CHIPS:, CH_DEV * q : CH_DEV * q + LANES]
        turned.append(jnp.concatenate([yr * tr - yi * ti, yr * ti + yi * tr], axis=1))
    high, low = halves(jnp.concatenate(turned, axis=0))
    wave = mm(high, tables[2]) + mm(high, tables[3]) + mm(low, tables[2])
    shape = (CHIPS, 2 * LANES)
    lane = lax.broadcasted_iota(jnp.int32, shape, 1) % LANES
    index = lax.broadcasted_iota(jnp.int32, shape, 0) + CHIPS * lane
    signed = jnp.where(index < NCH // 2, index, index - NCH)
    reach = jnp.where(index < NCH, jnp.abs(signed), NCH)
    kept = []
    for q in range(HALF_SEQS):
        limit = limit_ref[(2 * h + q // M_DEV) * CHIPS + column]
        kept.append(jnp.where(reach <= limit, wave[CHIPS * q : CHIPS * (q + 1)], 0.0))
    high, low = halves(jnp.concatenate(kept, axis=0))
    back = mm(high, tables[4]) + mm(high, tables[5]) + mm(low, tables[4])
    real, imag = [], []
    for q in range(HALF_SEQS):
        ur = back[CHIPS * q : CHIPS * (q + 1), :LANES]
        ui = back[CHIPS * q : CHIPS * (q + 1), LANES:]
        real.append(ur * tr + ui * ti)
        imag.append(ui * tr - ur * ti)
    high, low = halves(
        jnp.concatenate([jnp.concatenate(real, axis=1), jnp.concatenate(imag, axis=1)], axis=0)
    )
    field = mm(tables[6], high) + mm(tables[6], low) + mm(tables[7], high)
    return (field * (1.0 / NCH)).astype(BF)


def hot_sources(source):
    chip = ((source.astype(F32) + 0.5) * (1.0 / CH_DEV)).astype(jnp.int32)
    inside = source - CH_DEV * chip
    rows = lax.broadcasted_iota(jnp.int32, (LANES, NVS), 0)
    hot_inside = jnp.where(rows == inside, 1.0, 0.0).astype(BF)
    hot_chip = jnp.where(rows == chip, 1.0, 0.0)
    return hot_inside, hot_chip


def source_rows(field, hot_inside, hot_chip):
    lines = []
    for q in range(HALF_SEQS):
        for part in range(2):
            block = field[CHIPS * part : CHIPS * (part + 1), LANES * q : LANES * (q + 1)]
            chosen = mm(block, hot_inside) * hot_chip
            lines.append(jnp.sum(chosen, axis=0, keepdims=True))
    return lines


def reorder(new, old):
    rows = lax.broadcasted_iota(jnp.int32, (CHIPS, CHIPS), 0)
    cols = lax.broadcasted_iota(jnp.int32, (CHIPS, CHIPS), 1)
    return jnp.where(cols == old(*new(rows)), 1.0, 0.0).astype(BF)


def filtered_kernel(records, time_ref, limit_ref, src_ref, tables_hbm, twist_hbm, pick_hbm,
                    s_all, r_fin,
                    xbuf, tbuf, acc, tables, twist, pick,
                    a, g0, b0, x0, b1, g1, b2, x1, s_in, r_in, ry, rx,
                    in_sem, cz_s, cz_r, cp_s, cp_r, sz_s, sz_r, sx_s, sx_r, sy_s, sy_r,
                    ry_s, ry_r, rx_s, rx_r, rz_s, rz_r, here):
    seg = lax.axis_index("segment")
    chan = lax.axis_index("chan")
    z = lax.rem(chan, NZ)
    plane = lax.div(chan, NZ)
    x = lax.rem(plane, NX)
    y = lax.div(plane, NX)

    def zpeer(d, ds=0):
        return (lax.rem(seg + ds, SEG), plane * NZ + lax.rem(z + d, NZ))

    def ppeer(d):
        return (seg, lax.rem(plane + d, PLANE) * NZ + z)

    def xpeer(d):
        return (seg, (y * NX + lax.rem(x + d, NX)) * NZ + z)

    def ypeer(d):
        return (seg, (lax.rem(y + d, NY) * NX + x) * NZ + z)

    def remote(src, dst, send, recv, device):
        copy = pltpu.make_async_remote_copy(
            src_ref=src, dst_ref=dst, send_sem=send, recv_sem=recv,
            device_id=device, device_id_type=MESH,
        )
        copy.start()
        return copy

    def local(src, dst, sem):
        copy = pltpu.make_async_copy(src, dst, sem)
        copy.start()
        return copy

    loads = []
    for k in range(STEPS):
        row = []
        for s in range(RADIX):
            row.append(local(
                records.at[pl.ds(M_DEV * seg, M_DEV), :, pl.ds(QUARTER * s + KBLOCK * k, KBLOCK)],
                xbuf.at[k, s], in_sem.at[k, s]))
        row.append(local(time_ref.at[k], tbuf.at[k], in_sem.at[k, RADIX]))
        loads.append(row)
    later = [local(tables_hbm, tables, in_sem.at[STEPS, 0]),
             local(twist_hbm, twist, in_sem.at[STEPS, 1]),
             local(pick_hbm, pick, in_sem.at[STEPS, 2])]

    peers = [zpeer(d, ds) for ds in range(SEG) for d in range(NZ) if d or ds]
    peers += [ppeer(d) for d in range(1, PLANE)]
    barrier = pltpu.get_barrier_semaphore()
    for peer in peers:
        pl.semaphore_signal(barrier, inc=1, device_id=peer, device_id_type=MESH)

    for k in range(STEPS):
        for copy in loads[k]:
            copy.wait()
        q0, q1, q2, q3 = [xbuf[k, s].reshape(ROWS, KBLOCK).astype(F32) for s in range(RADIX)]
        s02, s13, d02, d13 = q0 + q2, q1 + q3, (q0 - q2).astype(BF), (q1 - q3).astype(BF)
        whole, rest = halves(s02 + s13)
        turn = (s02 - s13).astype(BF)

        def part(n):
            return tbuf[k, :, n * KBLOCK : (n + 1) * KBLOCK]

        sums = (
            mm_nt(part(0), whole) + mm_nt(part(0), rest),
            mm_nt(part(2), d02) + mm_nt(part(3), d13),
            mm_nt(part(1), turn),
            mm_nt(part(4), d02) + mm_nt(part(5), d13),
        )
        for r in range(RADIX):
            if k == 0:
                acc[r] = sums[r]
            else:
                acc[r] += sums[r]
    spectra = acc[...] * (1.0 / math.sqrt(NT))
    power = jnp.sum(jnp.sum(spectra * spectra, axis=0), axis=0, keepdims=True) * (1.0 / NF)
    white = spectra * lax.rsqrt(power + epsilon)[None]
    group = CHIPS // RADIX
    for h in range(2):
        for r in range(RADIX):
            blocks = []
            for part_of in range(2):
                for f in (2 * h, 2 * h + 1):
                    at = part_of * CHIPS + f * group
                    blocks.append(white[r, at : at + group])
            joined = jnp.concatenate(blocks, axis=1).astype(BF)
            a[h, 2 * r : 2 * r + 2] = joined.reshape(2, PLANE, 2 * WIDE)

    pl.semaphore_wait(barrier, len(peers))

    def slot(t):
        return lax.rem(t, RADIX) * 2 + lax.div(t, RADIX)

    z0 = [remote(a.at[0, slot(lax.rem(z + d, NZ))], g0.at[z], cz_s.at[0, d], cz_r.at[0, d], zpeer(d))
          for d in range(1, NZ)]
    own_z0 = local(a.at[0, slot(z)], g0.at[z], here.at[0])
    to_plane = reorder(lambda r: (r % NZ, r // NZ),
                       lambda t, p: ((t % RADIX) * 2 + t // RADIX) * PLANE + p)
    b1[...] = mm(to_plane, a[1].reshape(CHIPS, 2 * WIDE)).astype(BF).reshape(PLANE, NZ, 2 * WIDE)
    p1 = [remote(b1.at[lax.rem(plane + d, PLANE)], g1.at[plane], cp_s.at[1, d], cp_r.at[1, d], ppeer(d))
          for d in range(1, PLANE)]
    own_p1 = local(b1.at[plane], g1.at[plane], here.at[1])
    to_z = reorder(lambda r: (r % PLANE, r // PLANE), lambda p, t: p * NZ + t)
    own_p1.wait()
    for copy in p1:
        copy.wait_recv()
    b2[...] = mm(to_z, g1[...].reshape(CHIPS, 2 * WIDE)).astype(BF).reshape(NZ, PLANE, 2 * WIDE)
    z1 = [remote(b2.at[lax.rem(z + d, NZ)], x1.at[z], cz_s.at[1, d], cz_r.at[1, d], zpeer(d))
          for d in range(1, NZ)]
    own_z1 = local(b2.at[z], x1.at[z], here.at[2])
    from_z = reorder(lambda r: (r % NZ, r // NZ), lambda t, p: t * PLANE + p)
    own_z0.wait()
    for copy in z0:
        copy.wait_recv()
    b0[...] = mm(from_z, g0[...].reshape(CHIPS, 2 * WIDE)).astype(BF).reshape(PLANE, NZ, 2 * WIDE)
    p0 = [remote(b0.at[lax.rem(plane + d, PLANE)], x0.at[plane], cp_s.at[0, d], cp_r.at[0, d], ppeer(d))
          for d in range(1, PLANE)]
    own_p0 = local(b0.at[plane], x0.at[plane], here.at[3])
    for copy in later:
        copy.wait()
    hot_inside, hot_chip = hot_sources(src_ref[...])
    own_p0.wait()
    for copy in p0:
        copy.wait_recv()
    field = filter_half(0, x0[...].reshape(CHIPS, 2 * WIDE), chan, limit_ref, tables, twist)
    lines = source_rows(field, hot_inside, hot_chip)
    receivers = mm(field[:CHIPS], pick[0, 0]) + mm(field[CHIPS:], pick[1, 0])
    own_z1.wait()
    for copy in z1:
        copy.wait_recv()
    field = filter_half(1, x1[...].reshape(CHIPS, 2 * WIDE), chan, limit_ref, tables, twist)
    lines += source_rows(field, hot_inside, hot_chip)
    receivers += mm(field[:CHIPS], pick[0, 1]) + mm(field[CHIPS:], pick[1, 1])
    found = jnp.concatenate(lines, axis=0).astype(BF)
    s_in[0] = found[:, :HALF]
    s_in[1] = found[:, HALF:]

    own_s = local(s_in.at[seg], s_all.at[seg, y, x, z], here.at[4])
    s_z = [remote(s_in.at[lax.rem(seg + ds, SEG)], s_all.at[seg, y, x, z],
                  sz_s.at[ds, d], sz_r.at[ds, d], zpeer(d, ds))
           for ds in range(SEG) for d in range(NZ) if d or ds]
    r_in[...] = receivers.reshape(NY, NX, NZ, 1, LANES)
    r_y = [remote(r_in.at[lax.rem(y + d, NY)], ry.at[y], ry_s.at[d], ry_r.at[d], ypeer(d))
           for d in range(1, NY)]
    own_y = local(r_in.at[y], ry.at[y], here.at[5])
    own_s.wait()
    for copy in s_z:
        copy.wait_recv()
    s_x = []
    for d in range(1, NX):
        s_x.append(remote(s_all.at[0, y, x], s_all.at[0, y, x],
                          sx_s.at[0, d], sx_r.at[0, d], xpeer(d)))
        s_x.append(remote(s_all.at[1, y, x], s_all.at[1, y, x],
                          sx_s.at[1, d], sx_r.at[1, d], ypeer(d)))
    own_y.wait()
    for copy in r_y:
        copy.wait_recv()
    r_x = [remote(ry.at[:, lax.rem(x + d, NX)], rx.at[:, x], rx_s.at[d], rx_r.at[d], xpeer(d))
           for d in range(1, NX)]
    own_x = local(ry.at[:, x], rx.at[:, x], here.at[6])
    for copy in s_x:
        copy.wait_recv()

    def piece(part_of, at, n):
        if part_of == 0:
            return s_all.at[0, at, pl.ds(2 * n, 2)]
        return s_all.at[1, pl.ds(2 * n, 2), at]

    ends = ((y, ypeer, NY), (x, xpeer, NX))
    ahead, behind, onward = [], [], []
    for n in range(2):
        for part_of in range(2):
            me, peer, size = ends[part_of]
            up, down = piece(part_of, me, n), piece(part_of, me, 1 - n)
            ahead.append(remote(up, up, sy_s.at[part_of, 0, n], sy_r.at[part_of, 0, n], peer(1)))
            behind.append(remote(down, down, sy_s.at[part_of, 1, n], sy_r.at[part_of, 1, n],
                                 peer(size - 1)))
    own_x.wait()
    for copy in r_x:
        copy.wait_recv()
    r_z = [remote(rx.at[:, :, lax.rem(z + d, NZ)], r_fin.at[seg, :, :, z],
                  rz_s.at[ds, d], rz_r.at[ds, d], zpeer(d, ds))
           for ds in range(SEG) for d in range(NZ) if d or ds]
    own_r = local(rx.at[:, :, z], r_fin.at[seg, :, :, z], here.at[7])
    for part_of in range(2):
        me, peer, size = ends[part_of]
        ahead[part_of].wait_recv()
        got = piece(part_of, lax.rem(me + size - 1, size), 0)
        onward.append(remote(got, got, sy_s.at[part_of, 2, 0], sy_r.at[part_of, 2, 0], peer(1)))
        behind[part_of].wait_recv()
        got = piece(part_of, lax.rem(me + 1, size), 1)
        onward.append(remote(got, got, sy_s.at[part_of, 2, 1], sy_r.at[part_of, 2, 1],
                             peer(size - 1)))
    own_r.wait()
    for copy in ahead[2:] + behind[2:] + onward + r_z:
        copy.wait_recv()
    for copy in z0 + p1 + z1 + p0 + s_z + r_y + s_x + r_x + ahead + behind + onward + r_z:
        copy.wait_send()


def filtered(records, limits, sources):
    tables, twist, pick = filter_tables()
    hbm = pl.BlockSpec(memory_space=pl.ANY)
    smem = pl.BlockSpec(memory_space=pltpu.SMEM)
    vmem = pl.BlockSpec(memory_space=pltpu.VMEM)
    dma = pltpu.SemaphoreType.DMA
    by_z = pltpu.VMEM((NZ, PLANE, 2 * WIDE), BF)
    by_plane = pltpu.VMEM((PLANE, NZ, 2 * WIDE), BF)
    grid_of = pltpu.VMEM((NY, NX, NZ, 1, LANES), F32)
    pick = pick.reshape(2, 2, HALF_SEQS * LANES, LANES)
    return pl.pallas_call(
        filtered_kernel,
        out_shape=(
            jax.ShapeDtypeStruct((SEG, NY, NX, NZ, 2 * SEQS, HALF), BF),
            jax.ShapeDtypeStruct((SEG, NY, NX, NZ, 1, LANES), F32),
        ),
        in_specs=[hbm, hbm, smem, vmem, hbm, hbm, hbm],
        out_specs=(vmem, vmem),
        scratch_shapes=[
            pltpu.VMEM((STEPS, RADIX, M_DEV, CH_DEV, KBLOCK), BF),
            pltpu.VMEM((STEPS, 2 * CHIPS, 6 * KBLOCK), BF),
            pltpu.VMEM((RADIX, 2 * CHIPS, ROWS), F32),
            pltpu.VMEM(tables.shape, BF),
            pltpu.VMEM(twist.shape, F32),
            pltpu.VMEM(pick.shape, BF),
            pltpu.VMEM((2, NZ, PLANE, 2 * WIDE), BF),
            by_z, by_plane, by_plane, by_plane, by_plane, by_z, by_z,
            pltpu.VMEM((SEG, 2 * SEQS, HALF), BF),
            grid_of, grid_of, grid_of,
            dma((STEPS + 1, RADIX + 1)),
            dma((2, NZ)), dma((2, NZ)), dma((2, PLANE)), dma((2, PLANE)),
            dma((SEG, NZ)), dma((SEG, NZ)), dma((2, NX)), dma((2, NX)),
            dma((2, 3, 2)), dma((2, 3, 2)),
            dma((NY,)), dma((NY,)), dma((NX,)), dma((NX,)), dma((SEG, NZ)), dma((SEG, NZ)),
            dma((8,)),
        ],
        compiler_params=pltpu.CompilerParams(
            collective_id=0, has_side_effects=True, vmem_limit_bytes=56 << 20
        ),
        cost_estimate=pl.CostEstimate(flops=6 << 30, bytes_accessed=12 << 20, transcendentals=0),
        name="filtered",
    )(
        records,
        jnp.asarray(time_tables()),
        limits,
        sources.reshape(1, NVS),
        jnp.asarray(tables),
        jnp.asarray(twist),
        jnp.asarray(pick),
    )

VBLOCK = 32


def correlate_kernel(s_ref, r_ref, lag_ref, out_ref, flat, st, rt, cross):
    step = pl.program_id(0)

    @pl.when(step == 0)
    def _():
        shape = (LANES, LANES)
        eye = lax.broadcasted_iota(jnp.int32, shape, 0) == lax.broadcasted_iota(jnp.int32, shape, 1)
        eye = jnp.where(eye, 1.0, 0.0).astype(BF)
        for h in range(SEG):
            rt[h] = mm_nt(eye, r_ref[h].astype(BF))
            flat[...] = s_ref[h].reshape(CHIPS * 2 * SEQS, HALF).astype(F32)
            for g in range(2 * SEQS):
                piece = flat[pl.ds(g, CHIPS, stride=2 * SEQS), :].astype(BF)
                st[h, g] = mm_nt(eye, piece)

    for f in range(F_DEV):
        rr, ri = [], []
        for h in range(SEG):
            for m in range(M_DEV):
                g = (f * M_DEV + m) * 2
                rr.append(rt[h, RECS * g : RECS * (g + 1)])
                ri.append(rt[h, RECS * (g + 1) : RECS * (g + 2)])

        def body(b, carry, f=f, rr=rr, ri=ri):
            rows = pl.ds(pl.multiple_of(step * VBLOCK + b * 8, 8), 8)
            cr = jnp.zeros((8, RECS, LANES), F32)
            ci = jnp.zeros((8, RECS, LANES), F32)
            for h in range(SEG):
                for m in range(M_DEV):
                    g = (f * M_DEV + m) * 2
                    sr = st[h, g, rows, :][:, None, :]
                    si = st[h, g + 1, rows, :][:, None, :]
                    r, i = rr[h * M_DEV + m][None], ri[h * M_DEV + m][None]
                    cr = cr + sr * r + si * i
                    ci = ci + sr * i - si * r
            to = pl.ds(pl.multiple_of(b * 8 * RECS, 8 * RECS), 8 * RECS)
            cross[to, f * LANES : (f + 1) * LANES] = cr.reshape(8 * RECS, LANES).astype(BF)
            cross[to, NF + f * LANES : NF + (f + 1) * LANES] = (
                ci.reshape(8 * RECS, LANES).astype(BF)
            )
            return carry

        lax.fori_loop(0, VBLOCK // 8, body, 0, unroll=True)
    result = mm(cross[...], lag_ref[...]) * (1.0 / math.sqrt(MB * NF))
    out_ref[...] = result.astype(BF).reshape(VBLOCK, RECS, LAGS)


def correlate(s_all, r_all):
    return pl.pallas_call(
        correlate_kernel,
        out_shape=jax.ShapeDtypeStruct((HALF, RECS, LAGS), BF),
        grid=(HALF // VBLOCK,),
        in_specs=[
            pl.BlockSpec((SEG, CHIPS, 2 * SEQS, HALF), lambda k: (0, 0, 0, 0)),
            pl.BlockSpec((SEG, CHIPS, LANES), lambda k: (0, 0, 0)),
            pl.BlockSpec((2 * NF, LAGS), lambda k: (0, 0)),
        ],
        out_specs=pl.BlockSpec((VBLOCK, RECS, LAGS), lambda k: (k, 0, 0)),
        scratch_shapes=[
            pltpu.VMEM((CHIPS * 2 * SEQS, HALF), F32),
            pltpu.VMEM((SEG, 2 * SEQS, HALF, CHIPS), F32),
            pltpu.VMEM((SEG, LANES, CHIPS), F32),
            pltpu.VMEM((VBLOCK * RECS, 2 * NF), BF),
        ],
        compiler_params=pltpu.CompilerParams(vmem_limit_bytes=40 << 20),
        cost_estimate=pl.CostEstimate(flops=3 << 30, bytes_accessed=4 << 20, transcendentals=0),
        name="correlate",
    )(s_all, r_all, jnp.asarray(lag_table()))


def shards(records, fan_limit, sources):
    s_all, r_all = filtered(records, fan_limit, sources)
    return correlate(
        s_all.reshape(SEG, CHIPS, 2 * SEQS, HALF), r_all.reshape(SEG, CHIPS, LANES)
    )


def solution(mesh):
    in_specs = (P(None, "chan", None), P(), P())
    out_specs = P("segment", "chan", None)
    return jax.shard_map(shards, mesh=mesh, in_specs=in_specs, out_specs=out_specs, check_vma=False)
```

time: 85.2 us -> 58.2 us (0.68)
  the two profiles are of different devices: /device:TPU:1 before, /device:TPU:8 now
where the time goes in v1:
time: 58.2 us; the launch traced here: 57.3 us
  Pallas kernels  55.1 us (95%)
  local copies, waits for them, and re-layouts  2.13 us (4%)
    pallas_call x1, Pallas kernels, filtered(): pl.pallas_call(filtered_kernel, out_shape=(jax.ShapeDtypeStruct((SEG, NY,...  48.1 us
    pallas_call x1, Pallas kernels, correlate(): pl.pallas_call(correlate_kernel, out_shape=jax.ShapeDtypeStruct((HALF, RE...  7.04 us
    unnamed x6, local copies, waits for them, and re-layouts  2.13 us

profile of v1, /device:TPU:8, one launch (start us, length us, event | category | flops | bytes accessed | tf_op | source)
XLA Modules:
  0.0 57.3 jit_solution(7654137019993615219)
XLA Ops:
  0.0 0.0 copy-start
  0.0 48.1 %filtered.1 = (bf16[2,4,4,8,16,128]{5,4,3,2,1,0:T(8,128)(2,1)}, f32[2,4,4,8,1,128]{5,4,3,2,1,0:T(1,128)}) custom-call(bf16[4,80,7680]{2,1,0:T(8,128)(2,1)} %records.1, bf16[3,256,3840]{2,1,0:T(8,128)(2,1)} %constant.10.clone.time_ref, s32[512]{0:T(512)} %limit_ref.1, s32[1,256]{1,0:T(1,128)} %bitcast.5, bf16[10,256,256]{2,1,0:T(8,128)(2,1)} %constant.11.clone.tables_hbm, ...), custom_call_target="tpu_custom_call" | custom-call | flops 6442450944 | bytes 12582912 | tf_op jit(solution)/shard_map/filtered/pallas_call | solution.py:410
  48.1 0.0 copy-done
  48.1 0.0 copy-start.1
  48.1 1.2 %copy-done.1 = bf16[2,4,4,8,16,128]{5,4,3,2,1,0:T(8,128)(2,1)S(1)} copy-done((bf16[2,4,4,8,16,128]{5,4,3,2,1,0:T(8,128)(2,1)S(1)}, bf16[2,4,4,8,16,128]{5,4,3,2,1,0:T(8,128)(2,1)}, u32[]{:S(2)}) %copy-start.1) | copy-done | bytes 1048600
  49.4 0.0 copy-start.2
  49.4 0.9 %copy-done.2 = f32[2,4,4,8,1,128]{5,4,3,2,1,0:T(1,128)S(1)} copy-done((f32[2,4,4,8,1,128]{5,4,3,2,1,0:T(1,128)S(1)}, f32[2,4,4,8,1,128]{5,4,3,2,1,0:T(1,128)}, u32[]{:S(2)}) %copy-start.2) | copy-done | bytes 131096
  50.3 7.0 %correlate.1 = bf16[128,8,512]{2,1,0:T(8,128)(2,1)} custom-call(bf16[2,128,16,128]{3,2,1,0:T(8,128)(2,1)S(1)} %bitcast.3, f32[2,128,128]{2,1,0:T(8,128)S(1)} %bitcast.4, bf16[1024,512]{1,0:T(8,128)(2,1)S(1)} %copy-done), custom_call_target="tpu_custom_call" | custom-call | flops 3221225472 | bytes 4194304 | tf_op jit(solution)/shard_map/correlate/pallas_call | solution.py:502
Async XLA Ops:
  0.0 48.1 %copy-start = (bf16[1024,512]{1,0:T(8,128)(2,1)S(1)}, bf16[1024,512]{1,0:T(8,128)(2,1)}, u32[]{:S(2)}) copy-start(bf16[1024,512]{1,0:T(8,128)(2,1)} %constant.14.clone.lag_ref) | copy-start | bytes 3145732
  48.1 1.2 %copy-start.1 = (bf16[2,4,4,8,16,128]{5,4,3,2,1,0:T(8,128)(2,1)S(1)}, bf16[2,4,4,8,16,128]{5,4,3,2,1,0:T(8,128)(2,1)}, u32[]{:S(2)}) copy-start(bf16[2,4,4,8,16,128]{5,4,3,2,1,0:T(8,128)(2,1)} %get-tuple-element.7) | copy-start | bytes 3145732
  49.4 0.9 %copy-start.2 = (f32[2,4,4,8,1,128]{5,4,3,2,1,0:T(1,128)S(1)}, f32[2,4,4,8,1,128]{5,4,3,2,1,0:T(1,128)}, u32[]{:S(2)}) copy-start(f32[2,4,4,8,1,128]{5,4,3,2,1,0:T(1,128)} %get-tuple-element.8) | copy-start | bytes 393220

commit v2 on v1

v2 whole, which is shorter than its diff:
```python
import functools
import math

import jax
import jax.numpy as jnp
import numpy as np
from jax import lax
from jax.experimental import pallas as pl
from jax.experimental.pallas import tpu as pltpu
from jax.sharding import PartitionSpec as P

NCH = 10240
NT = 7680
NF = 512
FLO = 32
NVS = 256
STRIDE = 10
LAGS = 512
MB = 4

epsilon = 1e-06

SEG = 2
NY, NX, NZ = 4, 4, 8
CHIPS = NY * NX * NZ
CH_DEV = NCH // CHIPS
F_DEV = NF // CHIPS
M_DEV = MB // SEG
SEQS = F_DEV * M_DEV
RECS = CH_DEV // STRIDE
VBLOCK = 32
HALF = NVS // SEG
LANES = 128
HALF_SEQS = SEQS // 2
WIDE = HALF_SEQS * CH_DEV
PLANE = NY * NX
RADIX = 4
STEPS = 5
QUARTER = NT // RADIX
KBLOCK = QUARTER // STEPS
ROWS = M_DEV * CH_DEV
MESH = pl.DeviceIdType.MESH
FAR_Z = sorted(range(1, NZ), key=lambda d: -min(d, NZ - d))
FAR_PLANE = sorted(
    range(1, NY * NX), key=lambda d: -min(d // NX, NY - d // NX) - min(d % NX, NX - d % NX)
)
BF = jnp.bfloat16
F32 = jnp.float32


def as_bf16(array):
    return np.asarray(array, np.float32).astype(jnp.bfloat16)


def split(array):
    high = as_bf16(array)
    low = as_bf16(np.asarray(array, np.float64) - high.astype(np.float64))
    return high, low


def time_tables():
    plane, late = np.meshgrid(np.arange(PLANE), np.arange(NZ // RADIX))
    chips = plane * NZ + RADIX * late
    bins = FLO + CHIPS * np.arange(F_DEV)[:, None] + chips.reshape(1, -1)
    times = np.arange(QUARTER, dtype=np.int64)
    tables = []
    for residue in range(RADIX):
        freqs = (bins + residue).reshape(-1)
        phase = times[:, None] * freqs[None, :] % NT
        angle = phase.astype(np.float32) * np.float32(2.0 * math.pi / NT)
        tables.append(np.concatenate([np.cos(angle), -np.sin(angle)], axis=1))
    table = np.stack(tables).reshape(RADIX, STEPS, KBLOCK, 2 * CHIPS)
    return as_bf16(table.transpose(1, 0, 2, 3))


def lag_table():
    lagged = np.arange(LAGS, dtype=np.int64) - LAGS // 2
    freqs = FLO + np.arange(NF, dtype=np.int64)
    phase = freqs[:, None] * lagged[None, :] % NT
    angle = phase.astype(np.float32) * np.float32(2.0 * math.pi / NT)
    return as_bf16(np.stack([np.cos(angle), -np.sin(angle)]).reshape(2, 2, NF // 2, LAGS)
                   .transpose(1, 0, 2, 3).reshape(2, NF, LAGS))


def roots(rows, cols, modulus):
    phase = np.arange(rows)[:, None] * np.arange(cols)[None, :] % modulus
    angle = phase * (2.0 * math.pi / modulus)
    return np.cos(angle), -np.sin(angle)


def filter_tables():
    dr, di = roots(CHIPS, CHIPS, CHIPS)
    er = np.zeros((LANES, LANES))
    ei = np.zeros((LANES, LANES))
    er[:CH_DEV, :CH_DEV], ei[:CH_DEV, :CH_DEV] = roots(CH_DEV, CH_DEV, CH_DEV)
    tr = np.zeros((CHIPS, LANES))
    ti = np.zeros((CHIPS, LANES))
    tr[:, :CH_DEV], ti[:, :CH_DEV] = roots(CHIPS, CH_DEV, NCH)
    outer = np.block([[dr, -di], [di, dr]])
    inner = np.block([[er, ei], [-ei, er]])
    inner_back = np.block([[er, -ei], [ei, er]])
    outer_back = np.block([[dr, di], [-di, dr]])
    major = np.arange(CHIPS).reshape(PLANE, NZ).T.reshape(-1)
    outer_z = np.block([[dr[:, major], -di[:, major]], [di[:, major], dr[:, major]]])
    order = (outer, inner, inner_back, outer_back, outer_z)
    tables = np.stack([t for m in order for t in split(m)])
    twist = np.stack([tr, ti]).astype(np.float32)
    pick = np.zeros((2, SEQS, LANES, LANES), np.float32)
    for part in range(2):
        for q in range(SEQS):
            for u in range(RECS):
                pick[part, q, STRIDE * u, (q * 2 + part) * RECS + u] = 1.0
    return tables, twist, as_bf16(pick.reshape(2, SEQS * LANES, LANES))


def mm(left, right):
    return jnp.dot(left, right, preferred_element_type=F32)


def mm_nt(left, right):
    return lax.dot_general(left, right, (((1,), (1,)), ((), ())), preferred_element_type=F32)


def halves(value):
    high = value.astype(BF)
    return high, (value - high.astype(F32)).astype(BF)


def filter_half(h, x, column, limit_ref, tables, twist):
    tail = jnp.zeros((CHIPS, LANES // 2), BF)
    xs = jnp.concatenate(
        [
            jnp.concatenate([x[:, :WIDE], tail], axis=1),
            jnp.concatenate([x[:, WIDE:], tail], axis=1),
        ],
        axis=0,
    )
    outer = 0 if h == 0 else 8
    first = mm(tables[outer], xs) + mm(tables[outer + 1], xs)
    tr, ti = twist[0], twist[1]
    turned = []
    for q in range(HALF_SEQS):
        yr = first[:CHIPS, CH_DEV * q : CH_DEV * q + LANES]
        yi = first[CHIPS:, CH_DEV * q : CH_DEV * q + LANES]
        turned.append(jnp.concatenate([yr * tr - yi * ti, yr * ti + yi * tr], axis=1))
    high, low = halves(jnp.concatenate(turned, axis=0))
    wave = mm(high, tables[2]) + mm(high, tables[3]) + mm(low, tables[2])
    shape = (CHIPS, 2 * LANES)
    lane = lax.broadcasted_iota(jnp.int32, shape, 1) % LANES
    index = lax.broadcasted_iota(jnp.int32, shape, 0) + CHIPS * lane
    signed = jnp.where(index < NCH // 2, index, index - NCH)
    reach = jnp.where(index < NCH, jnp.abs(signed), NCH)
    kept = []
    for q in range(HALF_SEQS):
        limit = limit_ref[0, (2 * h + q // M_DEV) * CHIPS + column]
        kept.append(jnp.where(reach <= limit, wave[CHIPS * q : CHIPS * (q + 1)], 0.0))
    high, low = halves(jnp.concatenate(kept, axis=0))
    back = mm(high, tables[4]) + mm(high, tables[5]) + mm(low, tables[4])
    real, imag = [], []
    for q in range(HALF_SEQS):
        ur = back[CHIPS * q : CHIPS * (q + 1), :LANES]
        ui = back[CHIPS * q : CHIPS * (q + 1), LANES:]
        real.append(ur * tr + ui * ti)
        imag.append(ui * tr - ur * ti)
    high, low = halves(
        jnp.concatenate([jnp.concatenate(real, axis=1), jnp.concatenate(imag, axis=1)], axis=0)
    )
    field = mm(tables[6], high) + mm(tables[6], low) + mm(tables[7], high)
    return (field * (1.0 / NCH)).astype(BF)


def hot_sources(source):
    chip = ((source.astype(F32) + 0.5) * (1.0 / CH_DEV)).astype(jnp.int32)
    inside = source - CH_DEV * chip
    rows = lax.broadcasted_iota(jnp.int32, (LANES, NVS), 0)
    hot_inside = jnp.where(rows == inside, 1.0, 0.0).astype(BF)
    hot_chip = jnp.where(rows == chip, 1.0, 0.0)
    return hot_inside, hot_chip


def source_rows(field, hot_inside, hot_chip):
    lines = []
    for q in range(HALF_SEQS):
        for part in range(2):
            block = field[CHIPS * part : CHIPS * (part + 1), LANES * q : LANES * (q + 1)]
            chosen = mm(block, hot_inside) * hot_chip
            lines.append(jnp.sum(chosen, axis=0, keepdims=True))
    return jnp.concatenate(lines, axis=0).astype(BF)


def reorder(new, old):
    rows = lax.broadcasted_iota(jnp.int32, (CHIPS, CHIPS), 0)
    cols = lax.broadcasted_iota(jnp.int32, (CHIPS, CHIPS), 1)
    return jnp.where(cols == old(*new(rows)), 1.0, 0.0).astype(BF)


def sources_across(h, s_all, flat, st, eye):
    lines = 2 * HALF_SEQS
    for g in range(SEG):
        flat[...] = s_all[h, g].reshape(CHIPS * lines, HALF).astype(F32)
        for n in range(lines):
            st[g, n] = mm_nt(eye, flat[pl.ds(n, CHIPS, stride=lines), :].astype(BF))


def correlate_half(h, st, rt, lag, cross, total, keep):
    blocks = HALF // VBLOCK

    def spread_block(b):
        for f in range(F_DEV // 2):
            rr, ri = [], []
            for g in range(SEG):
                for m in range(M_DEV):
                    at = (((2 * h + f) * M_DEV + m) * 2) * RECS
                    rr.append(rt[g, at : at + RECS])
                    ri.append(rt[g, at + RECS : at + 2 * RECS])
            for v in range(VBLOCK // 8):
                rows = slice(b * VBLOCK + v * 8, b * VBLOCK + v * 8 + 8)
                cr = jnp.zeros((8, RECS, LANES), F32)
                ci = jnp.zeros((8, RECS, LANES), F32)
                for g in range(SEG):
                    for m in range(M_DEV):
                        n = (f * M_DEV + m) * 2
                        sr = st[g, n, rows, :][:, None, :]
                        si = st[g, n + 1, rows, :][:, None, :]
                        r, i = rr[g * M_DEV + m][None], ri[g * M_DEV + m][None]
                        cr = cr + sr * r + si * i
                        ci = ci + sr * i - si * r
                to = slice(v * 8 * RECS, (v + 1) * 8 * RECS)
                cross[b, to, f * LANES : (f + 1) * LANES] = cr.reshape(8 * RECS, LANES).astype(BF)
                cross[b, to, NF // 2 + f * LANES : NF // 2 + (f + 1) * LANES] = (
                    ci.reshape(8 * RECS, LANES).astype(BF)
                )

    def lag_block(b):
        result = mm(cross[b], lag[h])
        if h == 0:
            total[b] = result
        else:
            keep(b, (result + total[b]) * (1.0 / math.sqrt(MB * NF)))

    for b in range(blocks):
        spread_block(b)
        if b:
            lag_block(b - 1)
    lag_block(blocks - 1)


def whole_kernel(records, time_ref, limit_hbm, src_hbm, tables_hbm, twist_hbm, pick_hbm,
                    lag_hbm, out_ref, s_all, r_fin, flat, st, rt, cross, total, lag,
                    limit_ref, src_ref, result_buf,
                    xbuf, tbuf, acc, tables, twist, pick,
                    a, g0, b0, x0, b1, g1, b2, x1, s_in, r_in, ry, rx,
                    in_sem, cz_s, cz_r, cp_s, cp_r, sz_s, sz_r, sx_s, sx_r,
                    ry_s, ry_r, rx_s, rx_r, rz_s, rz_r, here):
    seg = lax.axis_index("segment")
    chan = lax.axis_index("chan")
    z = lax.rem(chan, NZ)
    plane = lax.div(chan, NZ)
    x = lax.rem(plane, NX)
    y = lax.div(plane, NX)

    def zpeer(d, ds=0):
        return (lax.rem(seg + ds, SEG), plane * NZ + lax.rem(z + d, NZ))

    def ppeer(d):
        return (seg, lax.rem(plane + d, PLANE) * NZ + z)

    def xpeer(d):
        return (seg, (y * NX + lax.rem(x + d, NX)) * NZ + z)

    def ypeer(d):
        return (seg, (lax.rem(y + d, NY) * NX + x) * NZ + z)

    def remote(src, dst, send, recv, device):
        copy = pltpu.make_async_remote_copy(
            src_ref=src, dst_ref=dst, send_sem=send, recv_sem=recv,
            device_id=device, device_id_type=MESH,
        )
        copy.start()
        return copy

    def local(src, dst, sem):
        copy = pltpu.make_async_copy(src, dst, sem)
        copy.start()
        return copy

    loads = [local(records.at[pl.ds(M_DEV * seg, M_DEV), :, pl.ds(QUARTER * s, QUARTER)],
                   xbuf.at[s], in_sem.at[0, s]) for s in range(RADIX)]
    chunks = [local(time_ref.at[k], tbuf.at[k], in_sem.at[1, k]) for k in range(2)]

    peers = [zpeer(d, ds) for ds in range(SEG) for d in range(NZ) if d or ds]
    peers += [ppeer(d) for d in range(1, PLANE)]
    barrier = pltpu.get_barrier_semaphore()
    for peer in peers:
        pl.semaphore_signal(barrier, inc=1, device_id=peer, device_id_type=MESH)
    chunks += [local(time_ref.at[k], tbuf.at[k], in_sem.at[1, k]) for k in range(2, STEPS)]
    later = [local(tables_hbm, tables, in_sem.at[2, 0]), local(twist_hbm, twist, in_sem.at[2, 1]),
             local(pick_hbm, pick, in_sem.at[2, 2]), local(limit_hbm, limit_ref, in_sem.at[0, 4]),
             local(src_hbm, src_ref, in_sem.at[2, 4])]
    lag_load = local(lag_hbm, lag, in_sem.at[2, 3])
    for copy in loads:
        copy.wait()

    for k in range(STEPS):
        chunks[k].wait()
        q0, q1, q2, q3 = [
            xbuf[s, :, :, k * KBLOCK : (k + 1) * KBLOCK].reshape(ROWS, KBLOCK).astype(F32)
            for s in range(RADIX)
        ]
        s02, s13, d02, d13 = q0 + q2, q1 + q3, (q0 - q2).astype(BF), (q1 - q3).astype(BF)
        whole, rest = halves(s02 + s13)
        turn = (s02 - s13).astype(BF)
        sums = (
            mm(whole, tbuf[k, 0]) + mm(rest, tbuf[k, 0]),
            mm(turn, tbuf[k, 2]),
            mm(d02, tbuf[k, 1]),
            mm(d13, tbuf[k, 1]),
            mm(d02, tbuf[k, 3]),
            mm(d13, tbuf[k, 3]),
        )
        for n in range(6):
            if k == 0:
                acc[n] = sums[n]
            else:
                acc[n] += sums[n]

    def turned_by(n, sign):
        real = acc[n, :, :CHIPS] + sign * acc[n + 1, :, CHIPS:]
        imag = acc[n, :, CHIPS:] - sign * acc[n + 1, :, :CHIPS]
        return jnp.concatenate([real, imag], axis=1)

    scale = 1.0 / math.sqrt(NT)
    spectra = [v * scale for v in (acc[0], turned_by(2, 1.0), acc[1], turned_by(4, -1.0))]
    squares = sum(v * v for v in spectra)
    power = jnp.sum(squares, axis=1, keepdims=True) * (1.0 / NF)
    factor = lax.rsqrt(power + epsilon)
    rows = lax.broadcasted_iota(jnp.int32, (2 * CHIPS, 2 * CHIPS), 0)
    cols = lax.broadcasted_iota(jnp.int32, (2 * CHIPS, 2 * CHIPS), 1)
    eye = jnp.where(rows == cols, 1.0, 0.0).astype(BF)
    white = [mm_nt(eye, (v * factor).astype(BF)) for v in spectra]
    group = CHIPS // RADIX
    for h in range(2):
        for r in range(RADIX):
            blocks = []
            for part_of in range(2):
                for f in (2 * h, 2 * h + 1):
                    at = part_of * CHIPS + f * group
                    blocks.append(white[r][at : at + group])
            joined = jnp.concatenate(blocks, axis=1).astype(BF)
            a[h, 2 * r : 2 * r + 2] = joined.reshape(2, PLANE, 2 * WIDE)

    pl.semaphore_wait(barrier, len(peers))

    def slot(t):
        return lax.rem(t, RADIX) * 2 + lax.div(t, RADIX)

    z0 = [remote(a.at[0, slot(lax.rem(z + d, NZ))], g0.at[z], cz_s.at[0, d], cz_r.at[0, d], zpeer(d))
          for d in FAR_Z]
    own_z0 = local(a.at[0, slot(z)], g0.at[z], here.at[0])
    to_plane = reorder(lambda r: (r % NZ, r // NZ),
                       lambda t, p: ((t % RADIX) * 2 + t // RADIX) * PLANE + p)
    b1[...] = mm(to_plane, a[1].reshape(CHIPS, 2 * WIDE)).astype(BF).reshape(PLANE, NZ, 2 * WIDE)
    p1 = [remote(b1.at[lax.rem(plane + d, PLANE)], g1.at[plane], cp_s.at[1, d], cp_r.at[1, d], ppeer(d))
          for d in FAR_PLANE]
    own_p1 = local(b1.at[plane], g1.at[plane], here.at[1])
    to_z = reorder(lambda r: (r % PLANE, r // PLANE), lambda p, t: p * NZ + t)
    own_p1.wait()
    for copy in p1:
        copy.wait_recv()
    b2[...] = mm(to_z, g1[...].reshape(CHIPS, 2 * WIDE)).astype(BF).reshape(NZ, PLANE, 2 * WIDE)
    z1 = [remote(b2.at[lax.rem(z + d, NZ)], x1.at[z], cz_s.at[1, d], cz_r.at[1, d], zpeer(d))
          for d in FAR_Z]
    own_z1 = local(b2.at[z], x1.at[z], here.at[2])
    from_z = reorder(lambda r: (r % NZ, r // NZ), lambda t, p: t * PLANE + p)
    own_z0.wait()
    for copy in z0:
        copy.wait_recv()
    b0[...] = mm(from_z, g0[...].reshape(CHIPS, 2 * WIDE)).astype(BF).reshape(PLANE, NZ, 2 * WIDE)
    p0 = [remote(b0.at[lax.rem(plane + d, PLANE)], x0.at[plane], cp_s.at[0, d], cp_r.at[0, d], ppeer(d))
          for d in FAR_PLANE]
    own_p0 = local(b0.at[plane], x0.at[plane], here.at[3])
    for copy in later:
        copy.wait()
    hot_inside, hot_chip = hot_sources(src_ref[...])
    own_p0.wait()
    for copy in p0:
        copy.wait_recv()
    field = filter_half(0, x0[...].reshape(CHIPS, 2 * WIDE), chan, limit_ref, tables, twist)
    receivers = mm(field[:CHIPS], pick[0, 0]) + mm(field[CHIPS:], pick[1, 0])
    found = source_rows(field, hot_inside, hot_chip)
    s_in[0, 0] = found[:, :HALF]
    s_in[0, 1] = found[:, HALF:]

    def send_z(h):
        sent = [remote(s_in.at[h, lax.rem(seg + ds, SEG)], s_all.at[h, seg, y, x, z],
                       sz_s.at[h, ds, d], sz_r.at[h, ds, d], zpeer(d, ds))
                for d in FAR_Z + [0] for ds in range(SEG) if d or ds]
        return sent, local(s_in.at[h, seg], s_all.at[h, seg, y, x, z], here.at[4 + h])

    first_axis, second_axis = (xpeer, ypeer), (ypeer, xpeer)

    def block(h, p, d, e):
        if p == 0:
            return s_all.at[h, 0, lax.rem(y + e, NY), lax.rem(x + NX - d, NX)]
        return s_all.at[h, 1, lax.rem(y + NY - d, NY), lax.rem(x + e, NX)]

    def send_block(h, p, d, e, kind, device):
        one = block(h, p, d, e)
        return remote(one, one, sx_s.at[h, p, kind, d], sx_r.at[h, p, kind, d], device)

    def phase_own(h):
        along = [None] * 4
        for d in (2, 1, 3):
            along[d] = [remote(block(h, p, 0, 0), block(h, p, 0, 0), sx_s.at[h, p, 0, d],
                               sx_r.at[h, p, 0, d], first_axis[p](d)) for p in range(2)]
        up = [None] * 4
        down = [None] * 4
        up[0] = [send_block(h, p, 0, 0, 1, second_axis[p](1)) for p in range(2)]
        down[0] = [send_block(h, p, 0, 0, 2, second_axis[p](3)) for p in range(2)]
        return along, up, down

    def phase_across(h, along, up, down):
        for d in (1, 3, 2):
            up[d], down[d] = [], []
            for p in range(2):
                along[d][p].wait_recv()
                up[d].append(send_block(h, p, d, 0, 1, second_axis[p](1)))
                down[d].append(send_block(h, p, d, 0, 2, second_axis[p](3)))

    def phase_relay(h, up, down):
        relay = [None] * 4
        for d in (0, 1, 3, 2):
            relay[d] = []
            for p in range(2):
                if d % 2 == 0:
                    up[d][p].wait_recv()
                    relay[d].append(send_block(h, p, d, 3, 3, second_axis[p](1)))
                else:
                    down[d][p].wait_recv()
                    relay[d].append(send_block(h, p, d, 1, 3, second_axis[p](3)))
        return relay

    def phase_done(up, down, relay):
        for d in range(4):
            for p in range(2):
                (down if d % 2 == 0 else up)[d][p].wait_recv()
                relay[d][p].wait_recv()

    s_z0, own_s0 = send_z(0)
    own_z1.wait()
    for copy in z1:
        copy.wait_recv()
    field = filter_half(1, x1[...].reshape(CHIPS, 2 * WIDE), chan, limit_ref, tables, twist)
    found = source_rows(field, hot_inside, hot_chip)
    s_in[1, 0] = found[:, :HALF]
    s_in[1, 1] = found[:, HALF:]
    s_z1, own_s1 = send_z(1)
    receivers += mm(field[:CHIPS], pick[0, 1]) + mm(field[CHIPS:], pick[1, 1])
    r_in[...] = receivers.reshape(NY, NX, NZ, 1, LANES)
    r_y = [remote(r_in.at[lax.rem(y + d, NY)], ry.at[y], ry_s.at[d], ry_r.at[d], ypeer(d))
           for d in range(1, NY)]
    own_y = local(r_in.at[y], ry.at[y], here.at[6])
    own_s0.wait()
    for copy in s_z0:
        copy.wait_recv()
    along0, up0, down0 = phase_own(0)
    for copy in z0 + p1 + z1 + p0:
        copy.wait_send()
    own_y.wait()
    for copy in r_y:
        copy.wait_recv()
    r_x = [remote(ry.at[:, lax.rem(x + d, NX)], rx.at[:, x], rx_s.at[d], rx_r.at[d], xpeer(d))
           for d in range(1, NX)]
    own_x = local(ry.at[:, x], rx.at[:, x], here.at[7])
    phase_across(0, along0, up0, down0)
    own_s1.wait()
    for copy in s_z1:
        copy.wait_recv()
    along1, up1, down1 = phase_own(1)
    own_x.wait()
    for copy in r_x:
        copy.wait_recv()
    r_z = [remote(rx.at[:, :, lax.rem(z + d, NZ)], r_fin.at[seg, :, :, z],
                  rz_s.at[ds, d], rz_r.at[ds, d], zpeer(d, ds))
           for d in FAR_Z + [0] for ds in range(SEG) if d or ds]
    own_r = local(rx.at[:, :, z], r_fin.at[seg, :, :, z], here.at[8])
    relay0 = phase_relay(0, up0, down0)
    for copy in s_z0 + s_z1 + r_y + r_x:
        copy.wait_send()
    phase_across(1, along1, up1, down1)
    phase_done(up0, down0, relay0)
    small = eye[:LANES, :LANES]
    sources_across(0, s_all, flat, st, small)
    relay1 = phase_relay(1, up1, down1)
    own_r.wait()
    for copy in r_z:
        copy.wait_recv()
    for g in range(SEG):
        rt[g] = mm_nt(small, r_fin[g].reshape(CHIPS, LANES).astype(BF))
    lag_load.wait()
    correlate_half(0, st, rt, lag, cross, total, None)
    for copy in r_z:
        copy.wait_send()
    for row in along0[1:] + along1[1:] + up0 + down0 + relay0:
        for copy in row:
            copy.wait_send()
    phase_done(up1, down1, relay1)
    sources_across(1, s_all, flat, st, small)
    writes = []

    def keep(b, result):
        part = slice(b * VBLOCK, (b + 1) * VBLOCK)
        result_buf[part] = result.astype(BF).reshape(VBLOCK, RECS, LAGS)
        at = pl.ds(b * VBLOCK, VBLOCK)
        writes.append(local(result_buf.at[at], out_ref.at[at], here.at[9 + b]))

    correlate_half(1, st, rt, lag, cross, total, keep)
    for row in up1 + down1 + relay1:
        for copy in row:
            copy.wait_send()
    for copy in writes:
        copy.wait()


def correlations(records, limits, sources):
    tables, twist, pick = filter_tables()
    hbm = pl.BlockSpec(memory_space=pl.ANY)
    dma = pltpu.SemaphoreType.DMA
    by_z = pltpu.VMEM((NZ, PLANE, 2 * WIDE), BF)
    by_plane = pltpu.VMEM((PLANE, NZ, 2 * WIDE), BF)
    grid_of = pltpu.VMEM((NY, NX, NZ, 1, LANES), F32)
    pick = pick.reshape(2, 2, HALF_SEQS * LANES, LANES)
    return pl.pallas_call(
        whole_kernel,
        out_shape=jax.ShapeDtypeStruct((HALF, RECS, LAGS), BF),
        in_specs=[hbm] * 8,
        out_specs=hbm,
        scratch_shapes=[
            pltpu.VMEM((2, SEG, NY, NX, NZ, SEQS, HALF), BF),
            pltpu.VMEM((SEG, NY, NX, NZ, 1, LANES), F32),
            pltpu.VMEM((CHIPS * SEQS, HALF), F32),
            pltpu.VMEM((SEG, SEQS, HALF, CHIPS), F32),
            pltpu.VMEM((SEG, LANES, CHIPS), F32),
            pltpu.VMEM((HALF // VBLOCK, VBLOCK * RECS, NF), BF),
            pltpu.VMEM((HALF // VBLOCK, VBLOCK * RECS, LAGS), F32),
            pltpu.VMEM((2, NF, LAGS), BF),
            pltpu.SMEM((1, NF), jnp.int32),
            pltpu.VMEM((1, NVS), jnp.int32),
            pltpu.VMEM((HALF, RECS, LAGS), BF),
            pltpu.VMEM((RADIX, M_DEV, CH_DEV, QUARTER), BF),
            pltpu.VMEM((STEPS, RADIX, KBLOCK, 2 * CHIPS), BF),
            pltpu.VMEM((6, ROWS, 2 * CHIPS), F32),
            pltpu.VMEM(tables.shape, BF),
            pltpu.VMEM(twist.shape, F32),
            pltpu.VMEM(pick.shape, BF),
            pltpu.VMEM((2, NZ, PLANE, 2 * WIDE), BF),
            by_z, by_plane, by_plane, by_plane, by_plane, by_z, by_z,
            pltpu.VMEM((2, SEG, SEQS, HALF), BF),
            grid_of, grid_of, grid_of,
            dma((3, STEPS)),
            dma((2, NZ)), dma((2, NZ)), dma((2, PLANE)), dma((2, PLANE)),
            dma((2, SEG, NZ)), dma((2, SEG, NZ)), dma((2, 2, 4, NX)), dma((2, 2, 4, NX)),
            dma((NY,)), dma((NY,)), dma((NX,)), dma((NX,)), dma((SEG, NZ)), dma((SEG, NZ)),
            dma((9 + HALF // VBLOCK,)),
        ],
        compiler_params=pltpu.CompilerParams(
            collective_id=0, has_side_effects=True, vmem_limit_bytes=57 << 20
        ),
        cost_estimate=pl.CostEstimate(flops=6 << 30, bytes_accessed=12 << 20, transcendentals=0),
        name="correlations",
    )(
        records,
        jnp.asarray(time_tables()),
        limits.reshape(1, NF),
        sources.reshape(1, NVS),
        jnp.asarray(tables),
        jnp.asarray(twist),
        jnp.asarray(pick),
        jnp.asarray(lag_table()),
    )

def settle_kernel(from_ref, to_ref, held, sems):
    count = 4
    parts = [pl.ds(k * (HALF // count), HALF // count) for k in range(count)]
    into = [pltpu.make_async_copy(from_ref.at[p], held.at[p], sems.at[0, k])
            for k, p in enumerate(parts)]
    onto = [pltpu.make_async_copy(held.at[p], to_ref.at[p], sems.at[1, k])
            for k, p in enumerate(parts)]
    for copy in into:
        copy.start()
    for one, two in zip(into, onto):
        one.wait()
        two.start()
    for copy in onto:
        copy.wait()


def shards(records, limits, sources):
    result = correlations(records, limits, sources)
    hbm = pl.BlockSpec(memory_space=pl.ANY)
    return pl.pallas_call(
        settle_kernel,
        out_shape=jax.ShapeDtypeStruct(result.shape, result.dtype),
        in_specs=[hbm],
        out_specs=hbm,
        scratch_shapes=[
            pltpu.VMEM(result.shape, result.dtype), pltpu.SemaphoreType.DMA((2, 4))
        ],
        compiler_params=pltpu.CompilerParams(vmem_limit_bytes=57 << 20),
        name="settle",
    )(result)


def solution(mesh):
    in_specs = (P(None, "chan", None), P(), P())
    out_specs = P("segment", "chan", None)
    return jax.shard_map(shards, mesh=mesh, in_specs=in_specs, out_specs=out_specs, check_vma=False)
```

time: 58.2 us -> 52.2 us (0.90)
  Pallas kernels: 55.1 us -> 51.2 us
  local copies, waits for them, and re-layouts: 2.13 us -> 0 us
    pallas_call x2, Pallas kernels: 55.1 us -> 51.2 us  [the longest x1 49.2 us: correlations(): pl.pallas_call(whole_kernel, out_shape=jax.ShapeDtypeStruct((HALF, RECS,...]
    unnamed x6 -> x0, local copies, waits for them, and re-layouts: 2.13 us -> none
where the time goes in v2:
time: 52.2 us; the launch traced here: 51.3 us
  Pallas kernels  51.2 us (98%)
    pallas_call x1, Pallas kernels, correlations(): pl.pallas_call(whole_kernel, out_shape=jax.ShapeDtypeStruct((HALF, RECS,...  49.2 us
    pallas_call x1, Pallas kernels, shards(): pl.pallas_call(settle_kernel, out_shape=jax.ShapeDtypeStruct(result.shape...  1.98 us

profile of v2, /device:TPU:8, one launch (start us, length us, event | category | flops | bytes accessed | tf_op | source)
XLA Modules:
  0.0 51.3 jit_solution(9139095091523914034)
XLA Ops:
  0.0 49.2 %correlations.1.from_ref = bf16[128,8,512]{2,1,0:T(8,128)(2,1)} custom-call(bf16[4,80,7680]{2,1,0:T(8,128)(2,1)} %records.1, bf16[5,4,384,256]{3,2,1,0:T(8,128)(2,1)} %constant.10.clone.time_ref, s32[1,512]{1,0:T(1,128)} %bitcast.2, s32[1,256]{1,0:T(1,128)} %bitcast.3, bf16[10,256,256]{2,1,0:T(8,128)(2,1)} %constant.11.clone.tables_hbm, ...), custom_call_target="tpu_custom_call" | custom-call | flops 6442450944 | bytes 12582912 | tf_op jit(solution)/shard_map/correlations/pallas_call | solution.py:533
  49.2 2.0 %settle.1 = bf16[128,8,512]{2,1,0:T(8,128)(2,1)} custom-call(bf16[128,8,512]{2,1,0:T(8,128)(2,1)} %correlations.1.from_ref), custom_call_target="tpu_custom_call" | custom-call | tf_op jit(solution)/shard_map/settle/pallas_call | solution.py:601

commit v3 on v2

--- a/solution.py
+++ b/solution.py
@@ -105,12 +105,12 @@
     order = (outer, inner, inner_back, outer_back, outer_z)
     tables = np.stack([t for m in order for t in split(m)])
     twist = np.stack([tr, ti]).astype(np.float32)
-    pick = np.zeros((2, SEQS, LANES, LANES), np.float32)
+    pick = np.zeros((2, HALF_SEQS, LANES, LANES), np.float32)
     for part in range(2):
-        for q in range(SEQS):
+        for q in range(HALF_SEQS):
             for u in range(RECS):
                 pick[part, q, STRIDE * u, (q * 2 + part) * RECS + u] = 1.0
-    return tables, twist, as_bf16(pick.reshape(2, SEQS * LANES, LANES))
+    return tables, twist, as_bf16(pick.reshape(2, HALF_SEQS * LANES, LANES))
 
 
 def mm(left, right):
@@ -210,7 +210,7 @@
             rr, ri = [], []
             for g in range(SEG):
                 for m in range(M_DEV):
-                    at = (((2 * h + f) * M_DEV + m) * 2) * RECS
+                    at = ((f * M_DEV + m) * 2) * RECS
                     rr.append(rt[g, at : at + RECS])
                     ri.append(rt[g, at + RECS : at + 2 * RECS])
             for v in range(VBLOCK // 8):
@@ -250,8 +250,7 @@
                     limit_ref, src_ref, result_buf,
                     xbuf, tbuf, acc, tables, twist, pick,
                     a, g0, b0, x0, b1, g1, b2, x1, s_in, r_in, ry, rx,
-                    in_sem, cz_s, cz_r, cp_s, cp_r, sz_s, sz_r, sx_s, sx_r,
-                    ry_s, ry_r, rx_s, rx_r, rz_s, rz_r, here):
+                    in_sem, late_sem, come, gone, pass_sem):
     seg = lax.axis_index("segment")
     chan = lax.axis_index("chan")
     z = lax.rem(chan, NZ)
@@ -284,25 +283,34 @@
         copy.start()
         return copy
 
-    loads = [local(records.at[pl.ds(M_DEV * seg, M_DEV), :, pl.ds(QUARTER * s, QUARTER)],
-                   xbuf.at[s], in_sem.at[0, s]) for s in range(RADIX)]
-    chunks = [local(time_ref.at[k], tbuf.at[k], in_sem.at[1, k]) for k in range(2)]
+    def settled(ref, sem):
+        pltpu.make_async_copy(ref, ref, sem).wait()
+
+    def fetch(k):
+        span = slice(k * KBLOCK, (k + 1) * KBLOCK)
+        for s in range(RADIX):
+            local(records.at[pl.ds(M_DEV * seg, M_DEV), :, pl.ds(QUARTER * s + KBLOCK * k, KBLOCK)],
+                  xbuf.at[s, :, :, span], in_sem.at[0, k])
+        local(time_ref.at[k], tbuf.at[k], in_sem.at[1, k])
+
+    fetch(0)
+    fetch(1)
 
     peers = [zpeer(d, ds) for ds in range(SEG) for d in range(NZ) if d or ds]
     peers += [ppeer(d) for d in range(1, PLANE)]
     barrier = pltpu.get_barrier_semaphore()
     for peer in peers:
         pl.semaphore_signal(barrier, inc=1, device_id=peer, device_id_type=MESH)
-    chunks += [local(time_ref.at[k], tbuf.at[k], in_sem.at[1, k]) for k in range(2, STEPS)]
-    later = [local(tables_hbm, tables, in_sem.at[2, 0]), local(twist_hbm, twist, in_sem.at[2, 1]),
-             local(pick_hbm, pick, in_sem.at[2, 2]), local(limit_hbm, limit_ref, in_sem.at[0, 4]),
-             local(src_hbm, src_ref, in_sem.at[2, 4])]
-    lag_load = local(lag_hbm, lag, in_sem.at[2, 3])
-    for copy in loads:
-        copy.wait()
+    for k in range(2, STEPS):
+        fetch(k)
+    later = [local(tables_hbm, tables, late_sem.at[0]), local(twist_hbm, twist, late_sem.at[1]),
+             local(pick_hbm, pick, late_sem.at[2]), local(limit_hbm, limit_ref, late_sem.at[3]),
+             local(src_hbm, src_ref, late_sem.at[4])]
+    lag_load = local(lag_hbm, lag, late_sem.at[5])
 
     for k in range(STEPS):
-        chunks[k].wait()
+        settled(xbuf.at[:, :, :, k * KBLOCK : (k + 1) * KBLOCK], in_sem.at[0, k])
+        settled(tbuf.at[k], in_sem.at[1, k])
         q0, q1, q2, q3 = [
             xbuf[s, :, :, k * KBLOCK : (k + 1) * KBLOCK].reshape(ROWS, KBLOCK).astype(F32)
             for s in range(RADIX)
@@ -339,7 +347,8 @@
     eye = jnp.where(rows == cols, 1.0, 0.0).astype(BF)
     white = [mm_nt(eye, (v * factor).astype(BF)) for v in spectra]
     group = CHIPS // RADIX
-    for h in range(2):
+
+    def assemble(h):
         for r in range(RADIX):
             blocks = []
             for part_of in range(2):
@@ -349,53 +358,55 @@
             joined = jnp.concatenate(blocks, axis=1).astype(BF)
             a[h, 2 * r : 2 * r + 2] = joined.reshape(2, PLANE, 2 * WIDE)
 
-    pl.semaphore_wait(barrier, len(peers))
-
     def slot(t):
         return lax.rem(t, RADIX) * 2 + lax.div(t, RADIX)
 
-    z0 = [remote(a.at[0, slot(lax.rem(z + d, NZ))], g0.at[z], cz_s.at[0, d], cz_r.at[0, d], zpeer(d))
-          for d in FAR_Z]
-    own_z0 = local(a.at[0, slot(z)], g0.at[z], here.at[0])
+    assemble(0)
+    pl.semaphore_wait(barrier, len(peers))
+    def cross_z(source, target, n, index):
+        for d in FAR_Z:
+            remote(source.at[index(lax.rem(z + d, NZ))], target.at[z], gone.at[n], come.at[n], zpeer(d))
+        local(source.at[index(z)], target.at[z], come.at[n])
+
+    def cross_plane(source, target, n):
+        for d in FAR_PLANE:
+            remote(source.at[lax.rem(plane + d, PLANE)], target.at[plane], gone.at[n], come.at[n],
+                   ppeer(d))
+        local(source.at[plane], target.at[plane], come.at[n])
+
+    cross_z(a.at[0], g0, 0, slot)
+    assemble(1)
     to_plane = reorder(lambda r: (r % NZ, r // NZ),
                        lambda t, p: ((t % RADIX) * 2 + t // RADIX) * PLANE + p)
     b1[...] = mm(to_plane, a[1].reshape(CHIPS, 2 * WIDE)).astype(BF).reshape(PLANE, NZ, 2 * WIDE)
-    p1 = [remote(b1.at[lax.rem(plane + d, PLANE)], g1.at[plane], cp_s.at[1, d], cp_r.at[1, d], ppeer(d))
-          for d in FAR_PLANE]
-    own_p1 = local(b1.at[plane], g1.at[plane], here.at[1])
+    cross_plane(b1, g1, 1)
+    from_z = reorder(lambda r: (r % NZ, r // NZ), lambda t, p: t * PLANE + p)
     to_z = reorder(lambda r: (r % PLANE, r // PLANE), lambda p, t: p * NZ + t)
-    own_p1.wait()
-    for copy in p1:
-        copy.wait_recv()
+    settled(g0, come.at[0])
+    b0[...] = mm(from_z, g0[...].reshape(CHIPS, 2 * WIDE)).astype(BF).reshape(PLANE, NZ, 2 * WIDE)
+    cross_plane(b0, x0, 2)
+    settled(g1, come.at[1])
     b2[...] = mm(to_z, g1[...].reshape(CHIPS, 2 * WIDE)).astype(BF).reshape(NZ, PLANE, 2 * WIDE)
-    z1 = [remote(b2.at[lax.rem(z + d, NZ)], x1.at[z], cz_s.at[1, d], cz_r.at[1, d], zpeer(d))
-          for d in FAR_Z]
-    own_z1 = local(b2.at[z], x1.at[z], here.at[2])
-    from_z = reorder(lambda r: (r % NZ, r // NZ), lambda t, p: t * PLANE + p)
-    own_z0.wait()
-    for copy in z0:
-        copy.wait_recv()
-    b0[...] = mm(from_z, g0[...].reshape(CHIPS, 2 * WIDE)).astype(BF).reshape(PLANE, NZ, 2 * WIDE)
-    p0 = [remote(b0.at[lax.rem(plane + d, PLANE)], x0.at[plane], cp_s.at[0, d], cp_r.at[0, d], ppeer(d))
-          for d in FAR_PLANE]
-    own_p0 = local(b0.at[plane], x0.at[plane], here.at[3])
+    cross_z(b2, x1, 3, lambda t: t)
     for copy in later:
         copy.wait()
     hot_inside, hot_chip = hot_sources(src_ref[...])
-    own_p0.wait()
-    for copy in p0:
-        copy.wait_recv()
+    settled(x0, come.at[2])
     field = filter_half(0, x0[...].reshape(CHIPS, 2 * WIDE), chan, limit_ref, tables, twist)
-    receivers = mm(field[:CHIPS], pick[0, 0]) + mm(field[CHIPS:], pick[1, 0])
     found = source_rows(field, hot_inside, hot_chip)
     s_in[0, 0] = found[:, :HALF]
     s_in[0, 1] = found[:, HALF:]
 
     def send_z(h):
-        sent = [remote(s_in.at[h, lax.rem(seg + ds, SEG)], s_all.at[h, seg, y, x, z],
-                       sz_s.at[h, ds, d], sz_r.at[h, ds, d], zpeer(d, ds))
-                for d in FAR_Z + [0] for ds in range(SEG) if d or ds]
-        return sent, local(s_in.at[h, seg], s_all.at[h, seg, y, x, z], here.at[4 + h])
+        for d in FAR_Z + [0]:
+            for ds in range(SEG):
+                if d or ds:
+                    remote(s_in.at[h, lax.rem(seg + ds, SEG)], s_all.at[h, seg, y, x, z],
+                           gone.at[4 + h], come.at[4 + h], zpeer(d, ds))
+        local(s_in.at[h, seg], s_all.at[h, seg, y, x, z], come.at[4 + h])
+
+    def sent_z(h):
+        settled(b1.at[pl.ds(0, 3)], gone.at[4 + h])
 
     first_axis, second_axis = (xpeer, ypeer), (ypeer, xpeer)
 
@@ -406,13 +417,15 @@
 
     def send_block(h, p, d, e, kind, device):
         one = block(h, p, d, e)
-        return remote(one, one, sx_s.at[h, p, kind, d], sx_r.at[h, p, kind, d], device)
+        early = (kind == 1 and d % 2 == 0) or (kind == 2 and d % 2 == 1)
+        recv = pass_sem.at[1, h, p, d] if early else come.at[6 + h]
+        return remote(one, one, gone.at[(8 if kind == 3 else 6) + h], recv, device)
 
     def phase_own(h):
         along = [None] * 4
         for d in (2, 1, 3):
-            along[d] = [remote(block(h, p, 0, 0), block(h, p, 0, 0), sx_s.at[h, p, 0, d],
-                               sx_r.at[h, p, 0, d], first_axis[p](d)) for p in range(2)]
+            along[d] = [remote(block(h, p, 0, 0), block(h, p, 0, 0), gone.at[10 + h],
+                               pass_sem.at[0, h, p, d], first_axis[p](d)) for p in range(2)]
         up = [None] * 4
         down = [None] * 4
         up[0] = [send_block(h, p, 0, 0, 1, second_axis[p](1)) for p in range(2)]
@@ -428,98 +441,111 @@
                 down[d].append(send_block(h, p, d, 0, 2, second_axis[p](3)))
 
     def phase_relay(h, up, down):
-        relay = [None] * 4
         for d in (0, 1, 3, 2):
-            relay[d] = []
             for p in range(2):
                 if d % 2 == 0:
                     up[d][p].wait_recv()
-                    relay[d].append(send_block(h, p, d, 3, 3, second_axis[p](1)))
+                    send_block(h, p, d, 3, 3, second_axis[p](1))
                 else:
                     down[d][p].wait_recv()
-                    relay[d].append(send_block(h, p, d, 1, 3, second_axis[p](3)))
-        return relay
-
-    def phase_done(up, down, relay):
-        for d in range(4):
-            for p in range(2):
-                (down if d % 2 == 0 else up)[d][p].wait_recv()
-                relay[d][p].wait_recv()
-
-    s_z0, own_s0 = send_z(0)
-    own_z1.wait()
-    for copy in z1:
-        copy.wait_recv()
+                    send_block(h, p, d, 1, 3, second_axis[p](3))
+
+    def phase_done(h):
+        settled(s_all.at[h, 0], come.at[6 + h])
+
+    def phase_sent(h):
+        settled(s_all.at[h, 0], gone.at[6 + h])
+        settled(s_all.at[h, 0, pl.ds(0, 2)], gone.at[8 + h])
+        settled(s_all.at[h, :, pl.ds(0, 3), 0], gone.at[10 + h])
+
+    def receivers(h, field):
+        found = mm(field[:CHIPS], pick[0]) + mm(field[CHIPS:], pick[1])
+        r_in[h] = found.reshape(NY, NX, NZ, 1, LANES)
+
+    def r_send_y(h):
+        for d in (2, 1, 3):
+            remote(r_in.at[h, lax.rem(y + d, NY)], ry.at[h, y], gone.at[12 + h], come.at[8 + h], ypeer(d))
+        local(r_in.at[h, y], ry.at[h, y], come.at[8 + h])
+
+    def r_send_x(h):
+        settled(ry.at[h], come.at[8 + h])
+        for d in (2, 1, 3):
+            remote(ry.at[h, :, lax.rem(x + d, NX)], rx.at[h, :, x], gone.at[14 + h], come.at[10 + h],
+                   xpeer(d))
+        local(ry.at[h, :, x], rx.at[h, :, x], come.at[10 + h])
+
+    def r_send_z(h):
+        settled(rx.at[h], come.at[10 + h])
+        for d in FAR_Z + [0]:
+            for ds in range(SEG):
+                if d or ds:
+                    remote(rx.at[h, :, :, lax.rem(z + d, NZ)], r_fin.at[h, seg, :, :, z],
+                           gone.at[16 + h], come.at[12 + h], zpeer(d, ds))
+        local(rx.at[h, :, :, z], r_fin.at[h, seg, :, :, z], come.at[12 + h])
+
+    def r_sent(h):
+        settled(r_in.at[h, pl.ds(0, 3)], gone.at[12 + h])
+        settled(ry.at[h, :, pl.ds(0, 3)], gone.at[14 + h])
+
+    def receivers_across(h):
+        for g in range(SEG):
+            rt[g] = mm_nt(small, r_fin[h, g].reshape(CHIPS, LANES).astype(BF))
+
+    small = eye[:LANES, :LANES]
+    send_z(0)
+    receivers(0, field)
+    r_send_y(0)
+    settled(x1, come.at[3])
     field = filter_half(1, x1[...].reshape(CHIPS, 2 * WIDE), chan, limit_ref, tables, twist)
     found = source_rows(field, hot_inside, hot_chip)
     s_in[1, 0] = found[:, :HALF]
     s_in[1, 1] = found[:, HALF:]
-    s_z1, own_s1 = send_z(1)
-    receivers += mm(field[:CHIPS], pick[0, 1]) + mm(field[CHIPS:], pick[1, 1])
-    r_in[...] = receivers.reshape(NY, NX, NZ, 1, LANES)
-    r_y = [remote(r_in.at[lax.rem(y + d, NY)], ry.at[y], ry_s.at[d], ry_r.at[d], ypeer(d))
-           for d in range(1, NY)]
-    own_y = local(r_in.at[y], ry.at[y], here.at[6])
-    own_s0.wait()
-    for copy in s_z0:
-        copy.wait_recv()
+    send_z(1)
+    receivers(1, field)
+    r_send_y(1)
+    r_send_x(0)
+    settled(s_all.at[0, 0, 0, pl.ds(0, 2)], come.at[4])
     along0, up0, down0 = phase_own(0)
-    for copy in z0 + p1 + z1 + p0:
-        copy.wait_send()
-    own_y.wait()
-    for copy in r_y:
-        copy.wait_recv()
-    r_x = [remote(ry.at[:, lax.rem(x + d, NX)], rx.at[:, x], rx_s.at[d], rx_r.at[d], xpeer(d))
-           for d in range(1, NX)]
-    own_x = local(ry.at[:, x], rx.at[:, x], here.at[7])
+    settled(a.at[0, pl.ds(0, NZ - 1)], gone.at[0])
+    settled(b1.at[pl.ds(0, PLANE - 1)], gone.at[1])
+    settled(b0.at[pl.ds(0, PLANE - 1)], gone.at[2])
+    settled(b2.at[pl.ds(0, NZ - 1)], gone.at[3])
+    r_send_x(1)
+    r_send_z(0)
     phase_across(0, along0, up0, down0)
-    own_s1.wait()
-    for copy in s_z1:
-        copy.wait_recv()
+    settled(s_all.at[1, 0, 0, pl.ds(0, 2)], come.at[5])
     along1, up1, down1 = phase_own(1)
-    own_x.wait()
-    for copy in r_x:
-        copy.wait_recv()
-    r_z = [remote(rx.at[:, :, lax.rem(z + d, NZ)], r_fin.at[seg, :, :, z],
-                  rz_s.at[ds, d], rz_r.at[ds, d], zpeer(d, ds))
-           for d in FAR_Z + [0] for ds in range(SEG) if d or ds]
-    own_r = local(rx.at[:, :, z], r_fin.at[seg, :, :, z], here.at[8])
-    relay0 = phase_relay(0, up0, down0)
-    for copy in s_z0 + s_z1 + r_y + r_x:
-        copy.wait_send()
+    r_send_z(1)
+    phase_relay(0, up0, down0)
+    sent_z(0)
+    sent_z(1)
+    r_sent(0)
+    r_sent(1)
     phase_across(1, along1, up1, down1)
-    phase_done(up0, down0, relay0)
-    small = eye[:LANES, :LANES]
+    phase_done(0)
     sources_across(0, s_all, flat, st, small)
-    relay1 = phase_relay(1, up1, down1)
-    own_r.wait()
-    for copy in r_z:
-        copy.wait_recv()
-    for g in range(SEG):
-        rt[g] = mm_nt(small, r_fin[g].reshape(CHIPS, LANES).astype(BF))
+    phase_relay(1, up1, down1)
+    settled(r_fin.at[0], come.at[12])
+    receivers_across(0)
     lag_load.wait()
     correlate_half(0, st, rt, lag, cross, total, None)
-    for copy in r_z:
-        copy.wait_send()
-    for row in along0[1:] + along1[1:] + up0 + down0 + relay0:
-        for copy in row:
-            copy.wait_send()
-    phase_done(up1, down1, relay1)
+    settled(b1.at[pl.ds(0, 12)], gone.at[16])
+    settled(b1.at[pl.ds(0, 12)], gone.at[17])
+    phase_sent(0)
+    settled(r_fin.at[1], come.at[13])
+    receivers_across(1)
+    phase_done(1)
     sources_across(1, s_all, flat, st, small)
-    writes = []
 
     def keep(b, result):
         part = slice(b * VBLOCK, (b + 1) * VBLOCK)
         result_buf[part] = result.astype(BF).reshape(VBLOCK, RECS, LAGS)
         at = pl.ds(b * VBLOCK, VBLOCK)
-        writes.append(local(result_buf.at[at], out_ref.at[at], here.at[9 + b]))
+        local(result_buf.at[at], out_ref.at[at], late_sem.at[6])
 
     correlate_half(1, st, rt, lag, cross, total, keep)
-    for row in up1 + down1 + relay1:
-        for copy in row:
-            copy.wait_send()
-    for copy in writes:
-        copy.wait()
+    phase_sent(1)
+    settled(result_buf, late_sem.at[6])
 
 
 def correlations(records, limits, sources):
@@ -528,8 +554,7 @@
     dma = pltpu.SemaphoreType.DMA
     by_z = pltpu.VMEM((NZ, PLANE, 2 * WIDE), BF)
     by_plane = pltpu.VMEM((PLANE, NZ, 2 * WIDE), BF)
-    grid_of = pltpu.VMEM((NY, NX, NZ, 1, LANES), F32)
-    pick = pick.reshape(2, 2, HALF_SEQS * LANES, LANES)
+    grid_of = pltpu.VMEM((2, NY, NX, NZ, 1, LANES), F32)
     return pl.pallas_call(
         whole_kernel,
         out_shape=jax.ShapeDtypeStruct((HALF, RECS, LAGS), BF),
@@ -537,7 +562,7 @@
         out_specs=hbm,
         scratch_shapes=[
             pltpu.VMEM((2, SEG, NY, NX, NZ, SEQS, HALF), BF),
-            pltpu.VMEM((SEG, NY, NX, NZ, 1, LANES), F32),
+            pltpu.VMEM((2, SEG, NY, NX, NZ, 1, LANES), F32),
             pltpu.VMEM((CHIPS * SEQS, HALF), F32),
             pltpu.VMEM((SEG, SEQS, HALF, CHIPS), F32),
             pltpu.VMEM((SEG, LANES, CHIPS), F32),
@@ -557,11 +582,7 @@
             by_z, by_plane, by_plane, by_plane, by_plane, by_z, by_z,
             pltpu.VMEM((2, SEG, SEQS, HALF), BF),
             grid_of, grid_of, grid_of,
-            dma((3, STEPS)),
-            dma((2, NZ)), dma((2, NZ)), dma((2, PLANE)), dma((2, PLANE)),
-            dma((2, SEG, NZ)), dma((2, SEG, NZ)), dma((2, 2, 4, NX)), dma((2, 2, 4, NX)),
-            dma((NY,)), dma((NY,)), dma((NX,)), dma((NX,)), dma((SEG, NZ)), dma((SEG, NZ)),
-            dma((9 + HALF // VBLOCK,)),
+            dma((2, STEPS)), dma((7,)), dma((14,)), dma((18,)), dma((2, 2, 2, NX)),
         ],
         compiler_params=pltpu.CompilerParams(
             collective_id=0, has_side_effects=True, vmem_limit_bytes=57 << 20

time: 52.2 us -> 48.8 us (0.935); the launches traced: 51.3 us -> 48.7 us
  Pallas kernels: 51.2 us -> 48.5 us
    pallas_call x1, Pallas kernels: 49.2 us -> 46.5 us  [correlations(): pl.pallas_call(whole_kernel, out_shape=jax.ShapeDtypeStruct((HALF, RECS,...]
where the time goes in v3:
time: 48.8 us; the launch traced here: 48.7 us
  Pallas kernels  48.5 us (99%)
    pallas_call x1, Pallas kernels, correlations(): pl.pallas_call(whole_kernel, out_shape=jax.ShapeDtypeStruct((HALF, RECS,...  46.5 us
    pallas_call x1, Pallas kernels, shards(): pl.pallas_call(settle_kernel, out_shape=jax.ShapeDtypeStruct(result.shape...  1.98 us

profile of v3, /device:TPU:8, one launch (start us, length us, event | category | flops | bytes accessed | tf_op | source)
XLA Modules:
  0.0 48.7 jit_solution(3518750862753099467)
XLA Ops:
  0.0 46.5 %correlations.1.from_ref = bf16[128,8,512]{2,1,0:T(8,128)(2,1)} custom-call(bf16[4,80,7680]{2,1,0:T(8,128)(2,1)} %records.1, bf16[5,4,384,256]{3,2,1,0:T(8,128)(2,1)} %constant.10.clone.time_ref, s32[1,512]{1,0:T(1,128)} %bitcast.2, s32[1,256]{1,0:T(1,128)} %bitcast.3, bf16[10,256,256]{2,1,0:T(8,128)(2,1)} %constant.11.clone.tables_hbm, ...), custom_call_target="tpu_custom_call" | custom-call | flops 6442450944 | bytes 12582912 | tf_op jit(solution)/shard_map/correlations/pallas_call | solution.py:558
  46.5 2.0 %settle.1 = bf16[128,8,512]{2,1,0:T(8,128)(2,1)} custom-call(bf16[128,8,512]{2,1,0:T(8,128)(2,1)} %correlations.1.from_ref), custom_call_target="tpu_custom_call" | custom-call | tf_op jit(solution)/shard_map/settle/pallas_call | solution.py:622

commit v4 on v3

--- a/solution.py
+++ b/solution.py
@@ -214,17 +214,23 @@
                     rr.append(rt[g, at : at + RECS])
                     ri.append(rt[g, at + RECS : at + 2 * RECS])
             for v in range(VBLOCK // 8):
-                rows = slice(b * VBLOCK + v * 8, b * VBLOCK + v * 8 + 8)
-                cr = jnp.zeros((8, RECS, LANES), F32)
-                ci = jnp.zeros((8, RECS, LANES), F32)
-                for g in range(SEG):
-                    for m in range(M_DEV):
-                        n = (f * M_DEV + m) * 2
-                        sr = st[g, n, rows, :][:, None, :]
-                        si = st[g, n + 1, rows, :][:, None, :]
-                        r, i = rr[g * M_DEV + m][None], ri[g * M_DEV + m][None]
-                        cr = cr + sr * r + si * i
-                        ci = ci + sr * i - si * r
+                crs, cis = [], []
+                for w in range(8):
+                    row = b * VBLOCK + v * 8 + w
+                    cr = ci = None
+                    for g in range(SEG):
+                        for m in range(M_DEV):
+                            n = (f * M_DEV + m) * 2
+                            sr = st[g, n, row : row + 1, :]
+                            si = st[g, n + 1, row : row + 1, :]
+                            r, i = rr[g * M_DEV + m], ri[g * M_DEV + m]
+                            one, two = sr * r + si * i, sr * i - si * r
+                            cr = one if cr is None else cr + one
+                            ci = two if ci is None else ci + two
+                    crs.append(cr)
+                    cis.append(ci)
+                cr = jnp.concatenate(crs, axis=0)
+                ci = jnp.concatenate(cis, axis=0)
                 to = slice(v * 8 * RECS, (v + 1) * 8 * RECS)
                 cross[b, to, f * LANES : (f + 1) * LANES] = cr.reshape(8 * RECS, LANES).astype(BF)
                 cross[b, to, NF // 2 + f * LANES : NF // 2 + (f + 1) * LANES] = (

time: 48.8 us -> 48.2 us (0.988)
  no operation moved by 1% of the time
where the time goes in v4:
time: 48.2 us; the launch traced here: 48.1 us
  Pallas kernels  48.1 us (100%)
    pallas_call x1, Pallas kernels, correlations(): pl.pallas_call(whole_kernel, out_shape=jax.ShapeDtypeStruct((HALF, RECS,...  46.2 us
    pallas_call x1, Pallas kernels, shards(): pl.pallas_call(settle_kernel, out_shape=jax.ShapeDtypeStruct(result.shape...  1.98 us

profile of v4, /device:TPU:8, one launch (start us, length us, event | category | flops | bytes accessed | tf_op | source)
XLA Modules:
  0.0 48.1 jit_solution(3222037432459085513)
XLA Ops:
  0.0 46.2 %correlations.1.from_ref = bf16[128,8,512]{2,1,0:T(8,128)(2,1)} custom-call(bf16[4,80,7680]{2,1,0:T(8,128)(2,1)} %records.1, bf16[5,4,384,256]{3,2,1,0:T(8,128)(2,1)} %constant.10.clone.time_ref, s32[1,512]{1,0:T(1,128)} %bitcast.2, s32[1,256]{1,0:T(1,128)} %bitcast.3, bf16[10,256,256]{2,1,0:T(8,128)(2,1)} %constant.11.clone.tables_hbm, ...), custom_call_target="tpu_custom_call" | custom-call | flops 6442450944 | bytes 12582912 | tf_op jit(solution)/shard_map/correlations/pallas_call | solution.py:564
  46.2 2.0 %settle.1 = bf16[128,8,512]{2,1,0:T(8,128)(2,1)} custom-call(bf16[128,8,512]{2,1,0:T(8,128)(2,1)} %correlations.1.from_ref), custom_call_target="tpu_custom_call" | custom-call | tf_op jit(solution)/shard_map/settle/pallas_call | solution.py:628

commit v5 on v4

--- a/solution.py
+++ b/solution.py
@@ -607,7 +607,7 @@
     )
 
 def settle_kernel(from_ref, to_ref, held, sems):
-    count = 4
+    count = 2
     parts = [pl.ds(k * (HALF // count), HALF // count) for k in range(count)]
     into = [pltpu.make_async_copy(from_ref.at[p], held.at[p], sems.at[0, k])
             for k, p in enumerate(parts)]
@@ -631,7 +631,7 @@
         in_specs=[hbm],
         out_specs=hbm,
         scratch_shapes=[
-            pltpu.VMEM(result.shape, result.dtype), pltpu.SemaphoreType.DMA((2, 4))
+            pltpu.VMEM(result.shape, result.dtype), pltpu.SemaphoreType.DMA((2, 2))
         ],
         compiler_params=pltpu.CompilerParams(vmem_limit_bytes=57 << 20),
         name="settle",

time: 48.2 us -> 48.3 us (level)
  no operation moved by 1% of the time
where the time goes in v5:
time: 48.3 us; the launch traced here: 48.2 us
  Pallas kernels  48.2 us (100%)
    pallas_call x1, Pallas kernels, correlations(): pl.pallas_call(whole_kernel, out_shape=jax.ShapeDtypeStruct((HALF, RECS,...  46.2 us
    pallas_call x1, Pallas kernels, shards(): pl.pallas_call(settle_kernel, out_shape=jax.ShapeDtypeStruct(result.shape...  2.04 us

profile of v5, /device:TPU:8, one launch (start us, length us, event | category | flops | bytes accessed | tf_op | source)
XLA Modules:
  0.0 48.2 jit_solution(4968909993549793357)
XLA Ops:
  0.0 46.2 %correlations.1.from_ref = bf16[128,8,512]{2,1,0:T(8,128)(2,1)} custom-call(bf16[4,80,7680]{2,1,0:T(8,128)(2,1)} %records.1, bf16[5,4,384,256]{3,2,1,0:T(8,128)(2,1)} %constant.10.clone.time_ref, s32[1,512]{1,0:T(1,128)} %bitcast.2, s32[1,256]{1,0:T(1,128)} %bitcast.3, bf16[10,256,256]{2,1,0:T(8,128)(2,1)} %constant.11.clone.tables_hbm, ...), custom_call_target="tpu_custom_call" | custom-call | flops 6442450944 | bytes 12582912 | tf_op jit(solution)/shard_map/correlations/pallas_call | solution.py:564
  46.2 2.0 %settle.1 = bf16[128,8,512]{2,1,0:T(8,128)(2,1)} custom-call(bf16[128,8,512]{2,1,0:T(8,128)(2,1)} %correlations.1.from_ref), custom_call_target="tpu_custom_call" | custom-call | tf_op jit(solution)/shard_map/settle/pallas_call | solution.py:628
